TPU v7x, 128 devices: a whole 4x4x4 slice. The times are simulated.
128 devices in a mesh: gz: 4 (over z), xy: 32 (over y, x, core).
Axes of the slice: x: 4, y: 4, z: 4, core: 2. Of those that a mesh axis runs over, the one named last changes fastest.
Arguments:
- features: bfloat16 [48, 16, 640, 256], P(None, 'gz', 'xy'), may hold values from -6 to 6
- first_weight: bfloat16 [3, 3, 3, 48, 48], replicated, may hold values from -0.15625 to 0.15625
- first_bias: float32 [48], replicated, may hold values from -0.5 to 0.5
- second_weight: bfloat16 [3, 3, 3, 64, 48], replicated, may hold values from -0.15625 to 0.15625
- second_bias: float32 [64], replicated, may hold values from -0.5 to 0.5
- labels: int32 [16, 640, 256], P('gz', 'xy'), may hold values from 0 to 16383, as said below
- blocks: int32 [4, 32, 256, 128], P('gz', 'xy'), may hold values from -1 to 20479, as said below
- owner_map: int32 [16384], replicated, may hold values from 0 to 16383, as said below
Outputs:
- mean_embedding: float32 [16384, 64], P(('gz', 'xy'))
- covariance: float32 [16384, 4096], P(('gz', 'xy'))
Inputs may be any that keep to these rules, and one draw needn't show every extreme that they name: `labels`: all voxels listed in one block carry the same label. A tile's 256 blocks together list every voxel of the tile exactly once. A block lists a quarter of 128 to 128 voxels whose indices follow one another in ascending order, then -1 to its end. In each tile at most 6 blocks have rows owner_map[label] within one device's 128 output rows, and in every draw the rows of some devices receive exactly 6 blocks from every tile. `owner_map`: A permutation of the output rows.
All inputs are finite; a program needn't handle non-finite values.
Results may differ from a plain program's by a relative error of at most 0.0042.
Values may be sent and summed in bfloat16 or wider, within the bound.
A program may use at most 128 MiB of HBM per device.

v0:
```python
import jax
import jax.numpy as jnp
from jax import lax
from jax.sharding import PartitionSpec as P

SV_DEV = 128


CONV_LAYOUT = ("NCDHW", "DHWOI", "NCDHW")


def extended(array, sides, width):
    for axis, dim in sides:
        devices, length = (lax.axis_size(axis), array.shape[dim])
        up = [(i, (i + 1) % devices) for i in range(devices - 1)]
        down = [(j, i) for i, j in up]
        last = lax.slice_in_dim(array, length - width, length, axis=dim)
        leading = lax.slice_in_dim(array, 0, width, axis=dim)
        before = lax.ppermute(last, axis, up)
        after = lax.ppermute(leading, axis, down)
        array = jnp.concatenate([before, array, after], axis=dim)
    return array


def convolve(padded, weight, bias):
    summed = lax.conv_general_dilated(
        padded[None],
        weight,
        (1, 1, 1),
        ((0, 0), (0, 0), (1, 1)),
        dimension_numbers=CONV_LAYOUT,
        preferred_element_type=jnp.float32,
    )[0]
    return summed + bias[:, None, None, None]


def pick_slots(values, slot_block, filler):
    extra = jnp.full((1,) + values.shape[1:], filler, values.dtype)
    return jnp.concatenate([values, extra], axis=0)[slot_block]


def local(
    features, first_weight, first_bias, second_weight, second_bias, labels, blocks, owner_map
):
    padded = extended(features, (("gz", 1), ("xy", 2)), 1)
    hidden = jax.nn.relu(convolve(padded, first_weight, first_bias)).astype(jnp.bfloat16)
    hidden_pad = extended(hidden, (("gz", 1), ("xy", 2)), 1)
    embedding = convolve(hidden_pad, second_weight, second_bias).astype(jnp.bfloat16)
    channels = embedding.shape[0]
    flat_embed = embedding.reshape(channels, -1)
    block_count = blocks.shape[2]
    block_width = blocks.shape[3]
    voxel_lists = blocks.reshape(block_count, block_width)
    in_block = voxel_lists >= 0
    picked = jnp.take(flat_embed, jnp.where(in_block, voxel_lists, 0).reshape(-1), axis=1).reshape(
        channels, block_count, block_width
    )
    picked = jnp.where(in_block[None], picked, jnp.zeros((), jnp.bfloat16))
    block_sizes = jnp.sum(in_block.astype(jnp.float32), axis=1)
    block_sums = jnp.einsum("cnk->nc", picked, preferred_element_type=jnp.float32)
    block_second = jnp.einsum(
        "cnk,dnk->ncd", picked, picked, preferred_element_type=jnp.float32
    ).reshape(block_count, channels * channels)
    owner_rows = owner_map[labels.reshape(-1)[voxel_lists[:, 0]]]
    depth_count = lax.axis_size("gz")
    plane_count = lax.axis_size("xy")
    devices = depth_count * plane_count
    capacity = max(2, 3 * block_count // devices)
    target_dev = owner_rows // SV_DEV
    local_rows = owner_rows % SV_DEV
    target_hits = (target_dev[:, None] == jnp.arange(devices, dtype=jnp.int32)[None, :]).astype(
        jnp.int32
    )
    slot_rank = jnp.sum((jnp.cumsum(target_hits, axis=0) - target_hits) * target_hits, axis=1)
    slot_block = (
        jnp.full((devices * capacity,), block_count, jnp.int32)
        .at[target_dev * capacity + slot_rank]
        .set(jnp.arange(block_count, dtype=jnp.int32))
    )
    send_sizes = pick_slots(block_sizes, slot_block, 0.0)
    send_rows = pick_slots(local_rows.astype(jnp.float32), slot_block, float(SV_DEV))
    send_sums = pick_slots(block_sums, slot_block, 0.0)
    send_second = pick_slots(block_second, slot_block, 0.0)
    moment_width = send_second.shape[1]
    arrived = (
        lax.all_to_all(
            send_sizes.reshape(devices, capacity),
            ("gz", "xy"),
            split_axis=0,
            concat_axis=0,
            tiled=True,
        ),
        lax.all_to_all(
            send_rows.reshape(devices, capacity),
            ("gz", "xy"),
            split_axis=0,
            concat_axis=0,
            tiled=True,
        ),
        lax.all_to_all(
            send_sums.reshape(devices, capacity, channels),
            ("gz", "xy"),
            split_axis=0,
            concat_axis=0,
            tiled=True,
        ),
        lax.all_to_all(
            send_second.reshape(devices, capacity, moment_width),
            ("gz", "xy"),
            split_axis=0,
            concat_axis=0,
            tiled=True,
        ),
    )
    got_sizes = arrived[0].reshape(devices * capacity)
    got_rows = arrived[1].reshape(devices * capacity).astype(jnp.int32)
    got_sums = arrived[2].reshape(devices * capacity, channels)
    got_second = arrived[3].reshape(devices * capacity, moment_width)
    row_hits = (got_rows[:, None] == jnp.arange(SV_DEV, dtype=jnp.int32)[None, :]).astype(
        jnp.float32
    )
    total_sizes = jnp.einsum("rs,r->s", row_hits, got_sizes, precision=lax.Precision.HIGHEST)
    total_sums = jnp.einsum("rs,rc->sc", row_hits, got_sums, precision=lax.Precision.HIGHEST)
    total_second = jnp.einsum("rs,rc->sc", row_hits, got_second, precision=lax.Precision.HIGHEST)
    denominator = jnp.maximum(total_sizes, 1.0)
    mean_embedding = total_sums / denominator[:, None]
    covariance = total_second / denominator[:, None] - (
        mean_embedding[:, :, None] * mean_embedding[:, None, :]
    ).reshape(SV_DEV, channels * channels)
    return (mean_embedding, covariance)


def solution(mesh):
    return jax.shard_map(
        local,
        mesh=mesh,
        in_specs=(
            P(None, "gz", "xy", None),
            P(),
            P(),
            P(),
            P(),
            P("gz", "xy", None),
            P("gz", "xy", None, None),
            P(),
        ),
        out_specs=(P(("gz", "xy"), None), P(("gz", "xy"), None)),
        check_vma=False,
    )
```

profile of v0, /device:TPU:20, one launch (start us, length us, event | category | flops | bytes accessed | tf_op | source)
XLA Modules:
  0.0 772.4 jit_solution(12519596503422814348)
XLA Ops:
  0.7 3.9 fusion.51
  4.6 0.9 copy.60
  5.5 1.3 collective-permute-start.1
  6.8 0.9 copy.59
  7.7 5.5 collective-permute-start
  13.4 1.7 gather_fusion
  15.2 1.7 gather_fusion.1
  17.5 1.4 scatter_custom_fusion
  19.0 5.0 gather_fusion.2
  24.7 10.6 %all-to-all-start = ((f32[128,1,6]{2,1,0:T(1,128)}), f32[128,1,6]{2,1,0:T(1,128)}, u32[]{:S(2)}, u32[]{:S(2)}) async-start(f32[128,1,6]{2,1,0:T(1,128)} %bitcast.11), calls=%async_computation | async-start | bytes 131072 | tf_op jit(solution)/shard_map/all_to_all | solution.py:93
  35.3 1.8 copy.43
  37.1 1.8 copy.42
  39.3 2.1 collective-permute-start.2
  41.3 3.8 collective-permute-start.3
  45.1 0.9 compare_select_fusion
  46.3 1.8 collective-permute-done.3
  48.0 3.4 maximum_bitcast_fusion
  51.4 5.6 pad.2
  57.0 19.5 %reshape.311 = bf16[48,6,22,1,8,33]{5,4,1,2,0,3:T(8,128)(2,1)} reshape(bf16[48,6,22,1,264]{4,1,2,0,3:T(8,128)(2,1)} %pad.2) | data formatting | bytes 6690816 | tf_op jit(solution)/shard_map/conv_general_dilated | solution.py:26
  76.5 18.3 %copy.46 = bf16[48,6,22,1,8,33]{0,4,5,2,1,3:T(8,128)(2,1)} copy(bf16[48,6,22,1,8,33]{5,4,1,2,0,3:T(8,128)(2,1)} %reshape.311) | data formatting | bytes 6690816 | tf_op jit(solution)/shard_map/conv_general_dilated | solution.py:26
  94.8 1.2 slice.64
  96.0 31.3 %broadcast_select_fusion.1 = f32[4,20,8,33,48]{4,2,3,1,0:T(8,128)} fusion(pred[8,33]{0,1:T(8,128)(4,1)S(1)} %copy-done.13, bf16[3,3,3,48,48]{4,3,2,1,0:T(8,128)(2,1)S(1)} %copy-done.12, bf16[48,6,22,1,7,2]{0,4,5,2,1,3:T(8,128)(2,1)S(1)} %slice.64, bf16[48,6,22,1,8,33]{0,4,5,2,1,3:T(8,128)(2,1)} %copy.46), kind=kOutput, calls=%fused_computation.28 | convolution fusion | flops 2639324160 | bytes 7702536 | tf_op jit(solution)/shard_map/conv_general_dilated | solution.py:26
  127.3 14.2 %copy.47 = f32[4,20,8,33,48]{3,2,4,1,0:T(8,128)} copy(f32[4,20,8,33,48]{4,2,3,1,0:T(8,128)} %broadcast_select_fusion.1) | data formatting | bytes 8110080 | tf_op jit(solution)/shard_map/conv_general_dilated | solution.py:26
  141.6 13.1 %reshape.222 = f32[4,20,1,264,48]{3,4,1,0,2:T(8,128)} reshape(f32[4,20,8,33,48]{3,2,4,1,0:T(8,128)} %copy.47) | data formatting | bytes 8110080 | tf_op jit(solution)/shard_map/conv_general_dilated | solution.py:26
  154.7 2.7 fusion.22
  157.4 3.7 collective-permute-start.4
  161.1 1.3 collective-permute-start.5
  162.5 9.8 %collective-permute-done.4 = bf16[48,1,20,256]{3,0,2,1:T(8,128)(2,1)S(1)} collective-permute-done((bf16[48,1,20,256]{3,0,2,1:T(8,128)(2,1)S(1)}, bf16[48,1,20,256]{3,0,2,1:T(8,128)(2,1)S(1)}, u32[]{:S(2)}, u32[]{:S(2)}) %collective-permute-start.4) | collective-permute-done | bytes 491552 | tf_op jit(solution)/shard_map/ppermute | solution.py:19
  172.2 4.6 collective-permute-done.5
  177.6 2.0 collective-permute-start.6
  179.6 3.5 collective-permute-start.7
  183.9 0.9 copy.38
  184.7 0.9 copy.39
  185.6 5.2 gather_fusion.5
  191.6 1.6 maximum_bitcast_fusion.1
  193.2 4.4 pad.4
  197.6 17.9 %reshape.225 = bf16[48,6,22,1,8,33]{5,4,0,2,1,3:T(8,128)(2,1)} reshape(bf16[48,6,22,1,264]{4,0,2,1,3:T(8,128)(2,1)} %pad.4) | data formatting | bytes 6690816 | tf_op jit(solution)/shard_map/conv_general_dilated | solution.py:26
  215.5 18.0 %copy.49 = bf16[48,6,22,1,8,33]{0,4,5,2,1,3:T(8,128)(2,1)} copy(bf16[48,6,22,1,8,33]{5,4,0,2,1,3:T(8,128)(2,1)} %reshape.225) | data formatting | bytes 6690816 | tf_op jit(solution)/shard_map/conv_general_dilated | solution.py:26
  233.6 1.2 slice.68
  234.8 29.6 %broadcast_select_fusion = f32[4,20,8,33,64]{4,2,3,1,0:T(8,128)S(1)} fusion(pred[8,33]{0,1:T(8,128)(4,1)S(1)} %copy-done.14, bf16[3,3,3,64,48]{3,4,2,1,0:T(8,128)(2,1)S(1)} %copy-done, bf16[48,6,22,1,7,2]{0,4,5,2,1,3:T(8,128)(2,1)S(1)} %slice.68, bf16[48,6,22,1,8,33]{0,4,5,2,1,3:T(8,128)(2,1)} %copy.49), kind=kOutput, calls=%fused_computation.27 | convolution fusion | flops 3515550720 | bytes 9095688 | tf_op jit(solution)/shard_map/conv_general_dilated | solution.py:26
  264.4 8.4 %copy.50 = f32[4,20,8,33,64]{4,0,3,2,1:T(4,128)} copy(f32[4,20,8,33,64]{4,2,3,1,0:T(8,128)S(1)} %broadcast_select_fusion) | data formatting | bytes 10813440 | tf_op jit(solution)/shard_map/conv_general_dilated | solution.py:26
  272.8 8.8 %slice_bitcast_fusion = f32[1,64,4,20,256]{1,2,4,3,0:T(4,128)} fusion(f32[4,20,1,264,64]{4,0,3,1,2:T(4,128)} %bitcast.91), kind=kLoop, calls=%fused_computation.11 | loop fusion | bytes 10485760 | tf_op jit(solution)/shard_map/conv_general_dilated | solution.py:26
  281.7 5.4 copy.51
  287.1 3.2 fusion.2
  290.3 112.7 %gather_fusion.3 = bf16[32768,64]{1,0:T(8,128)(2,1)} fusion(bf16[64,20480]{0,1:T(8,128)(2,1)} %fusion.2, s32[32768]{0:T(1024)S(1)} %broadcast_clamp_fusion), kind=kCustom, calls=%fused_computation.3 | custom fusion | bytes 8519680 | tf_op jit(solution)/shard_map/jit(_take)/gather | solution.py:55
  403.0 8.5 %copy.52 = bf16[64,256,128]{2,0,1:T(8,128)(2,1)} copy(bf16[64,256,128]{0,2,1:T(8,128)(2,1)} %bitcast.92) | data formatting | bytes 8388608 | tf_op jit(solution)/shard_map/jit(_take)/gather | solution.py:55
  411.5 9.8 %all-to-all-start.2 = ((f32[128,1,6]{2,1,0:T(1,128)}), f32[128,1,6]{2,1,0:T(1,128)S(1)}, u32[]{:S(2)}, u32[]{:S(2)}) async-start(f32[128,1,6]{2,1,0:T(1,128)} %bitcast.26), calls=%async_computation.2 | async-start | bytes 131072 | tf_op jit(solution)/shard_map/all_to_all | solution.py:86
  421.4 4.4 convert_reduce_fusion
  425.8 1.6 gather_fusion.4
  427.5 0.9 reshape.330
  428.4 9.8 %all-to-all-start.1 = ((f32[128,1,384]{2,1,0:T(1,128)}), f32[128,1,384]{2,1,0:T(1,128)S(1)}, u32[]{:S(2)}, u32[]{:S(2)}) async-start(f32[128,1,384]{2,1,0:T(1,128)} %reshape.330), calls=%async_computation.1 | async-start | bytes 393216 | tf_op jit(solution)/shard_map/all_to_all | solution.py:100
  438.2 9.0 %fusion.27 = f32[256,64,64]{2,1,0:T(8,128)} fusion(bf16[64,256,128]{2,0,1:T(8,128)(2,1)} %copy.52, pred[256,128]{1,0:T(8,128)(4,1)S(1)} %copy.39, pred[256,128]{1,0:T(8,128)(4,1)S(1)} %copy.38), kind=kOutput, calls=%fused_computation.40 | convolution fusion | flops 272629760 | bytes 8454144 | tf_op jit(solution)/shard_map/cnk,dnk->ncd/dot_general | solution.py:61
  447.2 7.8 %copy.54 = f32[256,64,64]{0,2,1:T(8,128)} copy(f32[256,64,64]{2,1,0:T(8,128)} %fusion.27) | data formatting | bytes 8388608 | tf_op jit(solution)/shard_map/cnk,dnk->ncd/dot_general | solution.py:61
  455.0 5.7 copy.55
  460.6 4.8 concatenate.31
  465.4 14.2 %gather_fusion.6 = f32[768,4096]{1,0:T(8,128)} fusion(f32[257,4096]{1,0:T(8,128)} %concatenate.31, s32[1024]{0:T(1024)S(1)} %pad_clamp_fusion), kind=kCustom, calls=%fused_computation.6 | custom fusion | bytes 25168896 | tf_op jit(solution)/shard_map/gather | solution.py:39
  479.6 13.9 %reshape.214 = f32[128,6,4096]{2,1,0:T(8,128)} reshape(f32[768,4096]{1,0:T(8,128)} %gather_fusion.6) | data formatting | bytes 25165824 | tf_op jit(solution)/shard_map/reshape | solution.py:108
  493.6 10.6 %all-to-all-start.3 = ((f32[128,6,4096]{2,1,0:T(8,128)}), f32[128,6,4096]{2,1,0:T(8,128)}, u32[]{:S(2)}, u32[]{:S(2)}) async-start(f32[128,6,4096]{2,1,0:T(8,128)} %reshape.214), calls=%async_computation.3 | async-start | bytes 33554432 | tf_op jit(solution)/shard_map/all_to_all | solution.py:107
  504.1 1.0 convert_reduce_fusion.2
  507.6 1.1 reduce.8
  509.8 1.8 copy.56
  511.6 235.0 %all-to-all-done.3 = f32[128,6,4096]{2,1,0:T(8,128)} async-done(((f32[128,6,4096]{2,1,0:T(8,128)}), f32[128,6,4096]{2,1,0:T(8,128)}, u32[]{:S(2)}, u32[]{:S(2)}) %all-to-all-start.3) | async-done | bytes 12582944 | tf_op jit(solution)/shard_map/all_to_all | solution.py:107
  746.6 14.8 %reshape.215 = f32[768,4096]{1,0:T(8,128)} reshape(f32[128,6,4096]{2,1,0:T(8,128)} %all-to-all-done.3) | data formatting | bytes 25165824 | tf_op jit(solution)/shard_map/reshape | solution.py:118
  761.4 10.8 %fusion.19 = f32[128,4096]{1,0:T(8,128)} fusion(f32[128,4096]{1,0:T(8,128)S(1)} %copy-done.4, f32[768,4096]{1,0:T(8,128)} %reshape.215, f32[128]{0:T(128)S(1)} %fusion.30, s32[768]{0:T(1024)S(1)} %convert_element_type.38), kind=kOutput, calls=%fused_computation.32 | convolution fusion | flops 4832985088 | bytes 16780800 | tf_op jit(solution)/shard_map/rs,rc->sc/dot_general | solution.py:124
  (83 shorter events, 8.0 us)
Async XLA Ops:
  0.6 234.1 %copy-start = (bf16[3,3,3,64,48]{3,4,2,1,0:T(8,128)(2,1)S(1)}, bf16[3,3,3,64,48]{3,4,2,1,0:T(8,128)(2,1)}, u32[]{:S(2)}) copy-start(bf16[3,3,3,64,48]{3,4,2,1,0:T(8,128)(2,1)} %param.11) | copy-start | bytes 497668
  0.6 12.6 %copy-start.9 = (s32[4,20,256]{2,0,1:T(4,128)S(1)}, s32[4,20,256]{2,0,1:T(4,128)}, u32[]{:S(2)}) copy-start(s32[4,20,256]{2,0,1:T(4,128)} %param.13) | copy-start | bytes 245764
  0.7 12.6 %copy-start.5 = (s32[1,1,256,128]{3,2,1,0:T(8,128)S(1)}, s32[1,1,256,128]{3,2,1,0:T(8,128)}, u32[]{:S(2)}) copy-start(s32[1,1,256,128]{3,2,1,0:T(8,128)} %param.14) | copy-start | bytes 393220
  0.7 14.5 %copy-start.3 = (s32[16384]{0:T(1024)S(1)}, s32[16384]{0:T(1024)}, u32[]{:S(2)}) copy-start(s32[16384]{0:T(1024)} %param.15) | copy-start | bytes 196612
  5.5 29.8 %collective-permute-start.1 = (bf16[48,1,20,256]{3,0,2,1:T(8,128)(2,1)}, bf16[48,1,20,256]{3,0,2,1:T(8,128)(2,1)}, u32[]{:S(2)}, u32[]{:S(2)}) collective-permute-start(bf16[48,1,20,256]{3,0,2,1:T(8,128)(2,1)} %copy.60), channel_id=1, source_target_pairs={{32,0},{64,32},{96,64},{33,1},{65,33},{97,65},{34,2},{66,34},{98,6... | collective-permute-start | bytes 1474568 | tf_op jit(solution)/shard_map/ppermute | solution.py:20
  7.7 31.2 %copy-start.2 = (bf16[48,4,20,256]{3,1,2,0:T(4,128)(2,1)S(1)}, bf16[48,4,20,256]{3,1,2,0:T(4,128)(2,1)}, u32[]{:S(2)}) copy-start(bf16[48,4,20,256]{3,1,2,0:T(4,128)(2,1)} %param.8) | copy-start | bytes 5898244
  7.7 29.4 %collective-permute-start = (bf16[48,1,20,256]{3,0,2,1:T(8,128)(2,1)}, bf16[48,1,20,256]{3,0,2,1:T(8,128)(2,1)}, u32[]{:S(2)}, u32[]{:S(2)}) collective-permute-start(bf16[48,1,20,256]{3,0,2,1:T(8,128)(2,1)} %copy.59), channel_id=1, source_target_pairs={{0,32},{32,64},{64,96},{1,33},{33,65},{65,97},{2,34},{34,66},{66,9... | collective-permute-start | bytes 1474568 | tf_op jit(solution)/shard_map/ppermute | solution.py:19
  24.7 386.8 %all-to-all-start = ((f32[128,1,6]{2,1,0:T(1,128)}), f32[128,1,6]{2,1,0:T(1,128)}, u32[]{:S(2)}, u32[]{:S(2)}) async-start(f32[128,1,6]{2,1,0:T(1,128)} %bitcast.11), calls=%async_computation | async-start | bytes 131072 | tf_op jit(solution)/shard_map/all_to_all | solution.py:93
  39.3 7.0 collective-permute-start.2
  41.3 6.7 collective-permute-start.3
  76.5 19.5 %copy-start.12 = (bf16[3,3,3,48,48]{4,3,2,1,0:T(8,128)(2,1)S(1)}, bf16[3,3,3,48,48]{4,3,2,1,0:T(8,128)(2,1)}, u32[]{:S(2)}) copy-start(bf16[3,3,3,48,48]{4,3,2,1,0:T(8,128)(2,1)} %param.9) | copy-start | bytes 373252
  76.5 19.6 %copy-start.13 = (pred[8,33]{0,1:T(8,128)(4,1)S(1)}, pred[8,33]{0,1:T(8,128)(4,1)}, u32[]{:S(2)}) copy-start(pred[8,33]{0,1:T(8,128)(4,1)} %constant.91) | copy-start | bytes 796
  141.6 13.1 %copy-start.11 = (f32[48]{0:T(128)S(1)}, f32[48]{0:T(128)}, u32[]{:S(2)}) copy-start(f32[48]{0:T(128)} %param.10) | copy-start | bytes 580
  154.7 7.8 %copy-start.6 = (s32[32768,1]{0,1:T(1,128)S(1)}, s32[32768,1]{0,1:T(1,128)}, u32[]{:S(2)}) copy-start(s32[32768,1]{0,1:T(1,128)} %compare_select_fusion) | copy-start | bytes 393220
  157.4 14.8 %collective-permute-start.4 = (bf16[48,1,20,256]{3,0,2,1:T(8,128)(2,1)S(1)}, bf16[48,1,20,256]{3,0,2,1:T(8,128)(2,1)S(1)}, u32[]{:S(2)}, u32[]{:S(2)}) collective-permute-start(bf16[48,1,20,256]{3,0,2,1:T(8,128)(2,1)S(1)} %get-tuple-element.8), channel_id=1, source_target_pairs={{0,32},{32,64},{64,96},{1,33},{33,65},{65,97},{2,34},{34,66},{66,9... | collective-permute-start | bytes 1474568 | tf_op jit(solution)/shard_map/ppermute | solution.py:19
  161.1 15.8 %collective-permute-start.5 = (bf16[48,1,20,256]{3,0,2,1:T(8,128)(2,1)S(1)}, bf16[48,1,20,256]{3,0,2,1:T(8,128)(2,1)S(1)}, u32[]{:S(2)}, u32[]{:S(2)}) collective-permute-start(bf16[48,1,20,256]{3,0,2,1:T(8,128)(2,1)S(1)} %get-tuple-element.9), channel_id=1, source_target_pairs={{32,0},{64,32},{96,64},{33,1},{65,33},{97,65},{34,2},{66,34},{98,6... | collective-permute-start | bytes 1474568 | tf_op jit(solution)/shard_map/ppermute | solution.py:20
  162.5 20.7 %copy-start.7 = (pred[256,128]{0,1:T(8,128)(4,1)}, pred[256,128]{0,1:T(8,128)(4,1)S(1)}, u32[]{:S(2)}) copy-start(pred[256,128]{0,1:T(8,128)(4,1)S(1)} %get-tuple-element.3) | copy-start | bytes 98308
  177.6 14.0 %collective-permute-start.6 = (bf16[48,6,1,256]{3,0,2,1:T(8,128)(2,1)}, bf16[48,6,1,256]{3,0,2,1:T(8,128)(2,1)}, u32[]{:S(2)}, u32[]{:S(2)}) collective-permute-start(bf16[48,6,1,256]{3,0,2,1:T(8,128)(2,1)} %get-tuple-element.6), channel_id=1, source_target_pairs={{0,1},{1,2},{2,3},{3,4},{4,5},{5,6},{6,7},{7,8},{8,9},{9,10},{10,1... | collective-permute-start | bytes 442376 | tf_op jit(solution)/shard_map/ppermute | solution.py:19
  179.6 12.0 %collective-permute-start.7 = (bf16[48,6,1,256]{3,0,2,1:T(8,128)(2,1)}, bf16[48,6,1,256]{3,0,2,1:T(8,128)(2,1)}, u32[]{:S(2)}, u32[]{:S(2)}) collective-permute-start(bf16[48,6,1,256]{3,0,2,1:T(8,128)(2,1)} %get-tuple-element.7), channel_id=1, source_target_pairs={{1,0},{2,1},{3,2},{4,3},{5,4},{6,5},{7,6},{8,7},{9,8},{10,9},{11,1... | collective-permute-start | bytes 442376 | tf_op jit(solution)/shard_map/ppermute | solution.py:20
  215.5 19.3 %copy-start.14 = (pred[8,33]{0,1:T(8,128)(4,1)S(1)}, pred[8,33]{0,1:T(8,128)(4,1)}, u32[]{:S(2)}) copy-start(pred[8,33]{0,1:T(8,128)(4,1)} %constant.91) | copy-start | bytes 796
  281.7 5.4 copy-start.10
  411.5 16.9 %all-to-all-start.2 = ((f32[128,1,6]{2,1,0:T(1,128)}), f32[128,1,6]{2,1,0:T(1,128)S(1)}, u32[]{:S(2)}, u32[]{:S(2)}) async-start(f32[128,1,6]{2,1,0:T(1,128)} %bitcast.26), calls=%async_computation.2 | async-start | bytes 131072 | tf_op jit(solution)/shard_map/all_to_all | solution.py:86
  428.4 65.1 %all-to-all-start.1 = ((f32[128,1,384]{2,1,0:T(1,128)}), f32[128,1,384]{2,1,0:T(1,128)S(1)}, u32[]{:S(2)}, u32[]{:S(2)}) async-start(f32[128,1,384]{2,1,0:T(1,128)} %reshape.330), calls=%async_computation.1 | async-start | bytes 393216 | tf_op jit(solution)/shard_map/all_to_all | solution.py:100
  493.6 253.1 %all-to-all-start.3 = ((f32[128,6,4096]{2,1,0:T(8,128)}), f32[128,6,4096]{2,1,0:T(8,128)}, u32[]{:S(2)}, u32[]{:S(2)}) async-start(f32[128,6,4096]{2,1,0:T(8,128)} %reshape.214), calls=%async_computation.3 | async-start | bytes 33554432 | tf_op jit(solution)/shard_map/all_to_all | solution.py:107
  509.6 251.9 %copy-start.8 = (f32[128,64]{0,1:T(8,128)}, f32[128,64]{0,1:T(8,128)S(1)}, u32[]{:S(2)}) copy-start(f32[128,64]{0,1:T(8,128)S(1)} %convolution_divide_fusion.1) | copy-start | bytes 98308
  511.6 249.8 %copy-start.4 = (f32[128,4096]{1,0:T(8,128)S(1)}, f32[128,4096]{1,0:T(8,128)}, u32[]{:S(2)}) copy-start(f32[128,4096]{1,0:T(8,128)} %copy.56) | copy-start | bytes 6291460
  746.6 25.6 %copy-start.1 = (bf16[3,3,3,64,48]{3,4,2,1,0:T(8,128)(2,1)S(1)}, bf16[3,3,3,64,48]{3,4,2,1,0:T(8,128)(2,1)}, u32[]{:S(2)}) copy-start(bf16[3,3,3,64,48]{3,4,2,1,0:T(8,128)(2,1)} %param.11) | copy-start | bytes 497668
where the time goes:
time: 782 us; the launch traced here: 772 us
  local copies, waits for them, and re-layouts  352 us (45%)
  waiting for transfers between devices  251 us (32%)
  matrix products  81.7 us (10%)
  starting transfers between devices  63.9 us (8%)
  other arithmetic  21.6 us (3%)
    all_to_all x1, waiting for transfers between devices, local(): lax.all_to_all(send_second.reshape(devices, capacity, moment_width), ('gz...  235 us
    conv_general_dilated x11, local copies, waits for them, and re-layouts, convolve(): lax.conv_general_dilated(padded[None], weight, (1, 1, 1), ((0, 0), (0, 0)...  126 us
    gather x2, local copies, waits for them, and re-layouts, local(): jnp.take(flat_embed, jnp.where(in_block, voxel_lists, 0).reshape(-1), axi...  121 us
    conv_general_dilated x2, matrix products, convolve(): lax.conv_general_dilated(padded[None], weight, (1, 1, 1), ((0, 0), (0, 0)...  60.9 us
    gather x4, local copies, waits for them, and re-layouts, pick_slots(): return jnp.concatenate([values, extra], axis=0)[slot_block]  26 us
  transfers between devices with their start and end apart: 12, of which 5 were waited for; matrix products, arithmetic and copies ran while one was open for 55% of the time, Pallas kernels for 0%

commit v1 on v0

v1 whole, which is shorter than its diff:
```python
import functools

import jax
import jax.numpy as jnp
from jax import lax
from jax.experimental import pallas as pl
from jax.experimental.pallas import tpu as pltpu
from jax.sharding import PartitionSpec as P

SV_DEV = 128
EMB = 64
HALF = 32
SLOTS = 6
PAIRS = 3
BODY = PAIRS * HALF
ROWS = BODY + 16
DEVS = 128
GROUPS = 160
MESH = pl.DeviceIdType.MESH

CONV_LAYOUT = ("NCDHW", "DHWOI", "NCDHW")


def extended(array, sides, width):
    for axis, dim in sides:
        devices, length = (lax.axis_size(axis), array.shape[dim])
        up = [(i, (i + 1) % devices) for i in range(devices - 1)]
        down = [(j, i) for i, j in up]
        last = lax.slice_in_dim(array, length - width, length, axis=dim)
        leading = lax.slice_in_dim(array, 0, width, axis=dim)
        before = lax.ppermute(last, axis, up)
        after = lax.ppermute(leading, axis, down)
        array = jnp.concatenate([before, array, after], axis=dim)
    return array


def convolve(padded, weight, bias):
    summed = lax.conv_general_dilated(
        padded[None],
        weight,
        (1, 1, 1),
        ((0, 0), (0, 0), (1, 1)),
        dimension_numbers=CONV_LAYOUT,
        preferred_element_type=jnp.float32,
    )[0]
    return summed + bias[:, None, None, None]


def table_kernel(blocks_ref, labels_ref, owner_ref, table_ref, held, scalars, used, sem):
    lists = blocks_ref[...]
    sizes = jnp.sum(jnp.where(lists >= 0, 1, 0), axis=1, keepdims=True)
    lane = lax.broadcasted_iota(jnp.int32, lists.shape, 1)
    both = jnp.where(lane == 0, lists, sizes).astype(jnp.float32)
    held[...] = both.T[0:8, :].astype(jnp.int32)
    copy = pltpu.make_async_copy(held, scalars, sem)
    copy.start()

    def clear_used(d, carry):
        used[d] = 0
        return carry

    def clear_table(d, carry):
        table_ref[d] = 0
        return carry

    lax.fori_loop(0, DEVS, clear_used, 0, unroll=8)
    lax.fori_loop(0, DEVS * SLOTS, clear_table, 0, unroll=8)
    copy.wait()

    def step(b, carry):
        start = scalars[0, b]
        size = scalars[1, b]
        line = start >> 8
        z = line // 20
        row = owner_ref[labels_ref[z, line - z * 20, start & 255]]
        device = row >> 7
        rank = used[device]
        used[device] = rank + 1
        table_ref[device * SLOTS + rank] = (start << 15) + (size << 7) + (row & 127)
        return carry

    lax.fori_loop(0, lists.shape[0], step, 0, unroll=4)


def slot_table(blocks, labels, owner_map):
    count = blocks.shape[0]
    return pl.pallas_call(
        table_kernel,
        out_shape=jax.ShapeDtypeStruct((DEVS * SLOTS,), jnp.int32),
        in_specs=[
            pl.BlockSpec(memory_space=pltpu.VMEM),
            pl.BlockSpec(memory_space=pltpu.SMEM),
            pl.BlockSpec(memory_space=pltpu.SMEM),
        ],
        out_specs=pl.BlockSpec(memory_space=pltpu.SMEM),
        scratch_shapes=[
            pltpu.VMEM((8, count), jnp.int32),
            pltpu.SMEM((8, count), jnp.int32),
            pltpu.SMEM((DEVS,), jnp.int32),
            pltpu.SemaphoreType.DMA,
        ],
    )(blocks, labels, owner_map)


def place(device):
    return (device // 32, lax.rem(device, 32))


def partner(me, k):
    core, x, y, z = lax.rem(me, 2), lax.rem(me // 2, 4), lax.rem(me // 8, 4), me // 32
    kc, kx, ky, kz = lax.rem(k, 2), lax.rem(k // 2, 4), lax.rem(k // 8, 4), k // 32
    ky = lax.rem(ky + kx, 4)
    kz = lax.rem(kz + kx + ky, 4)
    there = (lax.rem(z + kz, 4) * 4 + lax.rem(y + ky, 4)) * 4 + lax.rem(x + kx, 4)
    return there * 2 + lax.rem(core + kc, 2)


def moments_of(emb_ref, table_ref, device, send_ref):
    lane = lax.broadcasted_iota(jnp.int32, (1, 128), 1)
    inner = lax.broadcasted_iota(jnp.int32, (HALF, 128), 1) & 63
    outer = lax.broadcasted_iota(jnp.int32, (HALF, 128), 0)
    upper = (inner >= HALF) | (inner >= outer)
    diagonal = inner == outer
    line = lax.broadcasted_iota(jnp.int32, (16, 128), 0)
    zero = jnp.zeros((EMB, 256), jnp.bfloat16)
    one = jnp.ones((EMB, 256), jnp.bfloat16)
    extras = jnp.zeros((16, 128), jnp.float32)
    for p in range(PAIRS):
        lefts, rights, masks, sizes, rows = [], [], [], [], []
        for h in range(2):
            code = table_ref[device * SLOTS + 2 * p + h]
            start = code >> 15
            size = (code >> 7) & 255
            rows.append((code & 127).astype(jnp.float32))
            sizes.append(size.astype(jnp.float32))
            group = start >> 7
            low = start & 127
            first = emb_ref[group]
            second = emb_ref[jnp.minimum(group + 1, GROUPS - 1)]
            in_first = jnp.where((lane >= low) & (lane < low + size), 1.0, 0.0).astype(jnp.bfloat16)
            in_second = jnp.where(lane + 128 < low + size, 1.0, 0.0).astype(jnp.bfloat16)
            lefts += [first * in_first, second * in_second]
            masks += [in_first, in_second]
            rights.append(jnp.concatenate([first, second], axis=1))
        mask_rows = jnp.broadcast_to(jnp.concatenate(masks, axis=1), (16, 512))
        left = jnp.concatenate([jnp.concatenate(lefts, axis=1), mask_rows], axis=0)
        right = jnp.concatenate(
            [
                jnp.concatenate([rights[0], zero], axis=1),
                jnp.concatenate([zero, rights[1]], axis=1),
                jnp.concatenate([one, zero], axis=1),
                jnp.concatenate([zero, one], axis=1),
            ],
            axis=0,
        )
        result = lax.dot_general(
            left, right, (((1,), (1,)), ((), ())), preferred_element_type=jnp.float32
        )
        size_row = jnp.where(lane < EMB, sizes[0], sizes[1])
        owner_row = jnp.where(lane < EMB, rows[0], rows[1])
        mean = result[EMB : EMB + 1, 0:128] / jnp.maximum(size_row, 1.0)
        centred = result[0:EMB, 0:128] - result[0:EMB, 128:256] * mean
        rolled = pltpu.roll(centred[HALF:EMB], 96, 1)
        packed = jnp.where(upper, centred[0:HALF], rolled)
        send_ref[device, p * HALF : (p + 1) * HALF, :] = packed.astype(jnp.bfloat16)
        diag = jnp.sum(jnp.where(diagonal, rolled, 0.0), axis=0, keepdims=True)
        high = mean.astype(jnp.bfloat16).astype(jnp.float32)
        for place_of, value in (
            (p, diag),
            (3 + p, high),
            (6 + p, mean - high),
            (9 + p, size_row),
            (12 + p, owner_row),
        ):
            extras = jnp.where(line == place_of, value, extras)
    send_ref[device, BODY:ROWS, :] = extras.astype(jnp.bfloat16)


def exchange_kernel(emb_ref, table_ref, got_ref, send_ref, send_sem, recv_sem, own_sem):
    me = lax.axis_index("gz") * 32 + lax.axis_index("xy")
    barrier = pltpu.get_barrier_semaphore()

    def greet(k, carry):
        pl.semaphore_signal(
            barrier, inc=1, device_id=place(partner(me, k)), device_id_type=MESH
        )
        return carry

    lax.fori_loop(1, DEVS, greet, 0)
    moments_of(emb_ref, table_ref, me, send_ref)
    own = pltpu.make_async_copy(send_ref.at[me], got_ref.at[me], own_sem)
    own.start()
    pl.semaphore_wait(barrier, DEVS - 1)

    def copy(k):
        device = partner(me, k)
        return pltpu.make_async_remote_copy(
            src_ref=send_ref.at[device],
            dst_ref=got_ref.at[me],
            send_sem=send_sem.at[k],
            recv_sem=recv_sem.at[k],
            device_id=place(device),
            device_id_type=MESH,
        )

    def send(k, carry):
        moments_of(emb_ref, table_ref, partner(me, k), send_ref)
        copy(k).start()
        return carry

    lax.fori_loop(1, DEVS, send, 0)

    def finish(k, carry):
        copy(k).wait()
        return carry

    lax.fori_loop(1, DEVS, finish, 0)
    own.wait()


def exchange(embedding, table):
    return pl.pallas_call(
        exchange_kernel,
        out_shape=jax.ShapeDtypeStruct((DEVS, ROWS, 128), jnp.bfloat16),
        in_specs=[
            pl.BlockSpec(memory_space=pltpu.VMEM),
            pl.BlockSpec(memory_space=pltpu.SMEM),
        ],
        out_specs=pl.BlockSpec(memory_space=pl.ANY),
        scratch_shapes=[
            pltpu.VMEM((DEVS, ROWS, 128), jnp.bfloat16),
            pltpu.SemaphoreType.DMA((DEVS,)),
            pltpu.SemaphoreType.DMA((DEVS,)),
            pltpu.SemaphoreType.DMA,
        ],
        compiler_params=pltpu.CompilerParams(
            collective_id=0, has_side_effects=True, vmem_limit_bytes=40 << 20
        ),
    )(embedding, table)


CHUNKS = 4
QUAD = 4


def total_kernel(
    got_ref, mean_ref, cov_ref, body, extra, lines, acc_a, acc_b, id_vec, ids, hits, spread,
    second, full, body_sem, extra_sem, id_sem,
):
    fast = lax.Precision.HIGHEST
    per = DEVS // CHUNKS
    extra_copy = pltpu.make_async_copy(got_ref.at[:, pl.ds(BODY, 16), :], extra, extra_sem)
    extra_copy.start()
    body_copies = [
        pltpu.make_async_copy(
            got_ref.at[pl.ds(c * per, per), pl.ds(0, BODY), :],
            body.at[pl.ds(c * per, per)],
            body_sem.at[c],
        )
        for c in range(CHUNKS)
    ]
    for one in body_copies:
        one.start()
    acc_a[...] = jnp.zeros_like(acc_a)
    acc_b[...] = jnp.zeros_like(acc_b)
    extra_copy.wait()
    lines[...] = extra[...].astype(jnp.float32).reshape(DEVS * 16, 128)

    def line(k):
        return lines[pl.ds(k, DEVS, stride=16), :]

    lane = lax.broadcasted_iota(jnp.int32, (DEVS, 128), 1)
    row = lax.broadcasted_iota(jnp.int32, (DEVS, 128), 0)
    inner = lane & 63
    owners = [line(12 + p) for p in range(PAIRS)]
    id_vec[...] = jnp.where(
        inner == 0, owners[0], jnp.where(inner == 1, owners[1], owners[2])
    ).astype(jnp.int32)
    id_copy = pltpu.make_async_copy(id_vec, ids, id_sem)
    id_copy.start()

    means, sizes = [], []
    sums = jnp.zeros((DEVS, 384), jnp.float32)
    for p in range(PAIRS):
        mean = line(3 + p) + line(6 + p)
        size = line(9 + p)
        means.append(mean)
        sizes.append(size)
        turned = owners[p].T
        for h in range(2):
            hit = jnp.where(row == turned[64 * h : 64 * h + 1, :].astype(jnp.int32), 1.0, 0.0)
            hits[:, (2 * p + h) * 128 : (2 * p + h + 1) * 128] = hit
            mine = (lane >= EMB) if h else (lane < EMB)
            values = jnp.concatenate(
                [
                    jnp.where(mine, size * mean, 0.0),
                    jnp.where(mine, size, 0.0),
                    jnp.where(mine, line(p), 0.0),
                ],
                axis=1,
            )
            sums = sums + jnp.dot(
                hit, values, preferred_element_type=jnp.float32, precision=fast
            )

    def folded(value):
        return value + pltpu.roll(value, EMB, 1)

    count = jnp.maximum(folded(sums[:, 128:256]), 1.0)
    total_mean = folded(sums[:, 0:128]) / count
    mean_ref[...] = total_mean[:, 0:EMB]
    diag_sum = folded(sums[:, 256:384])
    inverse = 1.0 / count
    lines[0:DEVS, :] = diag_sum
    lines[DEVS : 2 * DEVS, :] = inverse

    for p in range(PAIRS):
        for h in range(2):
            owner = owners[p]
            other = pltpu.roll(owner, EMB, 1)
            owner_all = (
                jnp.where(lane < EMB, other, owner) if h else jnp.where(lane < EMB, owner, other)
            )
            hit_t = jnp.where(owner_all.astype(jnp.int32) == lane, 1.0, 0.0)
            theirs = jnp.dot(
                hit_t, total_mean, preferred_element_type=jnp.float32, precision=fast
            )
            off = jnp.sqrt(sizes[p]) * (means[p] - theirs)
            if h:
                off = pltpu.roll(off, EMB, 1)
            off = jnp.where(lane < EMB, off, 0.0)
            k = 2 * p + h
            second[k * 128 : (k + 1) * 128, :] = off.astype(jnp.bfloat16)
            spread[:, k * 128 : (k + 1) * 128] = off.T[0:EMB, :].astype(jnp.bfloat16)

    id_copy.wait()
    for c in range(CHUNKS):
        body_copies[c].wait()

        def add(s, carry):
            for p in range(PAIRS):
                value = body[s, p * HALF : (p + 1) * HALF, :].astype(jnp.float32)
                a = ids[s, p]
                b = ids[s, 64 + p]
                acc_a[a] = acc_a[a] + value
                acc_b[b] = acc_b[b] + value
            return carry

        lax.fori_loop(c * per, (c + 1) * per, add, 0, unroll=2)

    lane32 = lax.broadcasted_iota(jnp.int32, (HALF, 128), 1)
    row32 = lax.broadcasted_iota(jnp.int32, (HALF, 128), 0)

    def quad(q, carry):
        base = q * QUAD
        left = []
        for t in range(QUAD):
            mask = hits[pl.ds(base + t, 1), :].astype(jnp.bfloat16)
            left.append(spread[...] * mask)
        between = jnp.dot(
            jnp.concatenate(left, axis=0), second[...], preferred_element_type=jnp.float32
        )
        packed = [
            acc_a[base + t] + pltpu.roll(acc_b[base + t], EMB, 1) for t in range(QUAD)
        ]
        turned = jnp.concatenate(packed, axis=0).T
        for t in range(QUAD):
            diag = lines[pl.ds(base + t, 1), :]
            inv = lines[pl.ds(DEVS + base + t, 1), :]
            flip = pltpu.roll(turned, (128 - HALF * t) % 128, 1) if t else turned
            flip_up, flip_down = flip[0:HALF], flip[HALF:EMB]
            here = packed[t]
            top = jnp.where((lane32 >= HALF) | (lane32 >= row32), here, flip_up)
            low = jnp.where(
                lane32 < row32, here, jnp.where(lane32 == row32, diag, flip_up)
            )
            bottom = jnp.where(lane32 < HALF, flip_down, pltpu.roll(low, HALF, 1))
            both = jnp.concatenate([top, bottom], axis=0)
            both = (both + between[t * EMB : (t + 1) * EMB]) * inv
            full[pl.ds((base + t) * EMB, EMB), :] = both
        return carry

    lax.fori_loop(0, SV_DEV // QUAD, quad, 0)

    for t in range(EMB // 2):
        even = full[pl.ds(2 * t, SV_DEV, stride=EMB), :]
        odd = full[pl.ds(2 * t + 1, SV_DEV, stride=EMB), :]
        cov_ref[:, t * 128 : (t + 1) * 128] = jnp.where(
            lane < EMB, even, pltpu.roll(odd, EMB, 1)
        )


def totals(got):
    return pl.pallas_call(
        total_kernel,
        out_shape=(
            jax.ShapeDtypeStruct((SV_DEV, EMB), jnp.float32),
            jax.ShapeDtypeStruct((SV_DEV, EMB * EMB), jnp.float32),
        ),
        in_specs=[pl.BlockSpec(memory_space=pl.ANY)],
        out_specs=(
            pl.BlockSpec(memory_space=pltpu.VMEM),
            pl.BlockSpec(memory_space=pltpu.VMEM),
        ),
        scratch_shapes=[
            pltpu.VMEM((DEVS, BODY, 128), jnp.bfloat16),
            pltpu.VMEM((DEVS, 16, 128), jnp.bfloat16),
            pltpu.VMEM((DEVS * 16, 128), jnp.float32),
            pltpu.VMEM((SV_DEV, HALF, 128), jnp.float32),
            pltpu.VMEM((SV_DEV, HALF, 128), jnp.float32),
            pltpu.VMEM((DEVS, 128), jnp.int32),
            pltpu.SMEM((DEVS, 128), jnp.int32),
            pltpu.VMEM((SV_DEV, DEVS * SLOTS), jnp.float32),
            pltpu.VMEM((EMB, DEVS * SLOTS), jnp.bfloat16),
            pltpu.VMEM((DEVS * SLOTS, 128), jnp.bfloat16),
            pltpu.VMEM((SV_DEV * EMB, 128), jnp.float32),
            pltpu.SemaphoreType.DMA((CHUNKS,)),
            pltpu.SemaphoreType.DMA,
            pltpu.SemaphoreType.DMA,
        ],
        compiler_params=pltpu.CompilerParams(vmem_limit_bytes=48 << 20),
    )(got)


def local(
    features, first_weight, first_bias, second_weight, second_bias, labels, blocks, owner_map
):
    table = slot_table(blocks.reshape(blocks.shape[2], blocks.shape[3]), labels, owner_map)
    padded = extended(features, (("gz", 1), ("xy", 2)), 1)
    hidden = jax.nn.relu(convolve(padded, first_weight, first_bias)).astype(jnp.bfloat16)
    hidden_pad = extended(hidden, (("gz", 1), ("xy", 2)), 1)
    embedding = convolve(hidden_pad, second_weight, second_bias).astype(jnp.bfloat16)
    grouped = embedding.reshape(EMB, GROUPS, 128).transpose(1, 0, 2)
    return totals(exchange(grouped, table))


def solution(mesh):
    return jax.shard_map(
        local,
        mesh=mesh,
        in_specs=(
            P(None, "gz", "xy", None),
            P(),
            P(),
            P(),
            P(),
            P("gz", "xy", None),
            P("gz", "xy", None, None),
            P(),
        ),
        out_specs=(P(("gz", "xy"), None), P(("gz", "xy"), None)),
        check_vma=False,
    )
```

time: 782 us -> 569 us (0.73)
  the two profiles are of different devices: /device:TPU:20 before, /device:TPU:1 now
where the time goes in v1:
time: 569 us; the launch traced here: 560 us
  matrix products  287 us (50%)
  Pallas kernels  111 us (20%)
  local copies, waits for them, and re-layouts  98.8 us (17%)
  starting transfers between devices  24.1 us (4%)
  waiting for transfers between devices  23.1 us (4%)
  other arithmetic  14.5 us (3%)
    conv_general_dilated x2, matrix products, convolve(): lax.conv_general_dilated(padded[None], weight, (1, 1, 1), ((0, 0), (0, 0)...  287 us
    pallas_call x1, Pallas kernels, exchange(): pl.pallas_call(exchange_kernel, out_shape=jax.ShapeDtypeStruct((DEVS, ROW...  80.5 us
    broadcast_in_dim x2, local copies, waits for them, and re-layouts, convolve(): padded[None]  73.5 us
    pallas_call x1, Pallas kernels, totals(): pl.pallas_call(total_kernel, out_shape=(jax.ShapeDtypeStruct((SV_DEV, EMB...  21 us
    ppermute x4, starting transfers between devices, extended(): before = lax.ppermute(last, axis, up)  17.7 us
    ppermute x4, waiting for transfers between devices, extended(): after = lax.ppermute(leading, axis, down)  13.2 us
  transfers between devices with their start and end apart: 8, of which 6 were waited for; matrix products, arithmetic and copies ran while one was open for 1% of the time, Pallas kernels for 2%

profile of v1, /device:TPU:1, one launch (start us, length us, event | category | flops | bytes accessed | tf_op | source)
XLA Modules:
  0.0 560.0 jit_solution(289068295454272284)
XLA Ops:
  0.6 0.0 copy-start
  0.6 0.0 copy-start.3
  0.7 3.9 fusion.3
  4.5 0.1 copy.52
  4.7 4.4 collective-permute-start
  9.1 0.1 copy.53
  9.3 1.3 collective-permute-start.1
  10.6 8.4 %collective-permute-done = bf16[48,1,20,256]{3,0,2,1:T(8,128)(2,1)S(1)} collective-permute-done((bf16[48,1,20,256]{3,0,2,1:T(8,128)(2,1)S(1)}, bf16[48,1,20,256]{3,0,2,1:T(8,128)(2,1)S(1)}, u32[]{:S(2)}, u32[]{:S(2)}) %collective-permute-start) | collective-permute-done | bytes 491552 | tf_op jit(solution)/shard_map/ppermute | solution.py:31
  19.0 0.0 copy-done.3
  19.0 0.7 constant_dynamic-update-slice_fusion.1
  19.7 3.6 collective-permute-done.1
  23.3 4.7 collective-permute-start.2
  28.0 1.9 collective-permute-start.3
  30.0 0.2 collective-permute-done.2
  30.1 4.4 collective-permute-done.3
  34.5 2.1 maximum_bitcast_fusion
  36.6 0.0 copy-start.7
  36.6 36.8 %copy.40 = bf16[1,48,6,22,256]{1,0,4,3,2:T(2,128)(2,1)} copy(bf16[1,48,6,22,256]{4,1,3,2,0:T(8,128)(2,1)} %maximum_bitcast_fusion) | data formatting | bytes 6488064 | tf_op jit(solution)/shard_map/broadcast_in_dim | solution.py:39
  73.4 0.0 copy-done.7
  73.4 0.0 copy-start.5
  73.4 136.9 %fusion.4 = f32[1,48,4,20,256]{1,0,4,3,2:T(1,128)} fusion(bf16[1,48,6,22,256]{1,0,4,3,2:T(2,128)(2,1)} %copy.40, bf16[3,3,3,48,48]{4,3,2,1,0:T(8,128)(2,1)S(1)} %copy-done.7), kind=kOutput, calls=%fused_computation.14 | convolution fusion | flops 2541404160 | bytes 7300608 | tf_op jit(solution)/shard_map/conv_general_dilated | solution.py:38
  210.2 0.0 copy-done.5
  210.3 5.5 maximum_convert_fusion
  215.7 0.0 copy-start.2
  215.7 2.3 copy-done.2
  218.1 0.3 fusion.1
  218.4 1.3 copy.41
  219.6 3.4 collective-permute-start.4
  223.0 1.3 copy.42
  224.3 1.3 collective-permute-start.5
  225.6 4.7 copy.43
  230.3 0.0 copy-start.4
  230.3 1.3 collective-permute-done.4
  231.6 5.3 collective-permute-done.5
  236.9 0.7 pad_maximum_fusion.2
  237.6 5.2 collective-permute-start.6
  242.8 1.9 collective-permute-start.7
  244.7 0.0 copy-done.4
  244.7 0.6 copy.47.labels_ref
  245.4 9.9 %shard_map.95.table_ref = s32[768]{0:T(1024)} custom-call(s32[256,128]{1,0:T(8,128)} %bitcast.15, s32[4,20,256]{2,1,0:T(8,128)} %copy.47.labels_ref, s32[16384]{0:T(1024)} %owner_ref.1), custom_call_target="tpu_custom_call" | custom-call | tf_op jit(solution)/shard_map/pallas_call | solution.py:87
  255.3 0.0 collective-permute-done.6
  255.4 0.0 collective-permute-done.7
  255.4 2.9 maximum_bitcast_fusion.1
  258.2 36.7 %copy.44 = bf16[1,48,6,22,256]{1,0,4,3,2:T(2,128)(2,1)} copy(bf16[1,48,6,22,256]{4,1,3,2,0:T(8,128)(2,1)} %maximum_bitcast_fusion.1) | data formatting | bytes 6488064 | tf_op jit(solution)/shard_map/broadcast_in_dim | solution.py:39
  295.0 0.0 copy-done
  295.0 150.1 %fusion.5 = f32[1,64,4,20,256]{1,0,4,3,2:T(1,128)} fusion(bf16[1,48,6,22,256]{1,0,4,3,2:T(2,128)(2,1)} %copy.44, bf16[3,3,3,64,48]{3,4,2,1,0:T(8,128)(2,1)S(1)} %copy-done), kind=kOutput, calls=%fused_computation.15 | convolution fusion | flops 3388538880 | bytes 8652800 | tf_op jit(solution)/shard_map/conv_general_dilated | solution.py:38
  445.0 0.0 copy-start.6
  445.1 9.1 %copy.46 = f32[64,160,128]{2,0,1:T(8,128)} copy(f32[64,160,128]{0,2,1:T(8,128)} %bitcast.14) | data formatting | bytes 10485760 | tf_op jit(solution)/shard_map/squeeze | solution.py:38
  454.1 0.0 copy-done.6
  454.1 0.0 copy-start.1
  454.1 3.3 fusion.emb_ref
  457.4 0.0 copy-done.1
  457.4 80.5 %shard_map.96.got_ref = bf16[128,112,128]{2,1,0:T(8,128)(2,1)S(1)} custom-call(bf16[160,64,128]{2,1,0:T(8,128)(2,1)S(1)} %fusion.emb_ref, s32[768]{0:T(1024)S(1)} %copy-done.1), custom_call_target="tpu_custom_call" | custom-call | tf_op jit(solution)/shard_map/pallas_call | solution.py:222
  537.9 21.0 %shard_map.97 = (f32[128,64]{1,0:T(8,128)S(1)}, f32[128,4096]{1,0:T(8,128)}) custom-call(bf16[128,112,128]{2,1,0:T(8,128)(2,1)S(1)} %shard_map.96.got_ref), custom_call_target="tpu_custom_call" | custom-call | tf_op jit(solution)/shard_map/pallas_call | solution.py:394
  558.9 0.7 copy.48
  (3 shorter events, 0.1 us)
Async XLA Ops:
  0.6 294.4 %copy-start = (bf16[3,3,3,64,48]{3,4,2,1,0:T(8,128)(2,1)S(1)}, bf16[3,3,3,64,48]{3,4,2,1,0:T(8,128)(2,1)}, u32[]{:S(2)}) copy-start(bf16[3,3,3,64,48]{3,4,2,1,0:T(8,128)(2,1)} %param.11) | copy-start | bytes 497668
  0.6 18.3 %copy-start.3 = (bf16[48,4,20,256]{3,1,2,0:T(4,128)(2,1)S(1)}, bf16[48,4,20,256]{3,1,2,0:T(4,128)(2,1)}, u32[]{:S(2)}) copy-start(bf16[48,4,20,256]{3,1,2,0:T(4,128)(2,1)} %param.8) | copy-start | bytes 5898244
  4.7 14.3 %collective-permute-start = (bf16[48,1,20,256]{3,0,2,1:T(8,128)(2,1)S(1)}, bf16[48,1,20,256]{3,0,2,1:T(8,128)(2,1)S(1)}, u32[]{:S(2)}, u32[]{:S(2)}) collective-permute-start(bf16[48,1,20,256]{3,0,2,1:T(8,128)(2,1)S(1)} %copy.52), channel_id=1, source_target_pairs={{0,32},{32,64},{64,96},{1,33},{33,65},{65,97},{2,34},{34,66},{66,9... | collective-permute-start | bytes 1474568 | tf_op jit(solution)/shard_map/ppermute | solution.py:31
  9.3 14.0 %collective-permute-start.1 = (bf16[48,1,20,256]{3,0,2,1:T(8,128)(2,1)S(1)}, bf16[48,1,20,256]{3,0,2,1:T(8,128)(2,1)S(1)}, u32[]{:S(2)}, u32[]{:S(2)}) collective-permute-start(bf16[48,1,20,256]{3,0,2,1:T(8,128)(2,1)S(1)} %copy.53), channel_id=1, source_target_pairs={{32,0},{64,32},{96,64},{33,1},{65,33},{97,65},{34,2},{66,34},{98,6... | collective-permute-start | bytes 1474568 | tf_op jit(solution)/shard_map/ppermute | solution.py:32
  23.3 6.8 %collective-permute-start.2 = (bf16[48,6,1,256]{3,0,2,1:T(8,128)(2,1)S(1)}, bf16[48,6,1,256]{3,0,2,1:T(8,128)(2,1)S(1)}, u32[]{:S(2)}, u32[]{:S(2)}) collective-permute-start(bf16[48,6,1,256]{3,0,2,1:T(8,128)(2,1)S(1)} %get-tuple-element.14), channel_id=1, source_target_pairs={{0,1},{1,2},{2,3},{3,4},{4,5},{5,6},{6,7},{7,8},{8,9},{9,10},{10,1... | collective-permute-start | bytes 442376 | tf_op jit(solution)/shard_map/ppermute | solution.py:31
  28.0 6.5 %collective-permute-start.3 = (bf16[48,6,1,256]{3,0,2,1:T(8,128)(2,1)S(1)}, bf16[48,6,1,256]{3,0,2,1:T(8,128)(2,1)S(1)}, u32[]{:S(2)}, u32[]{:S(2)}) collective-permute-start(bf16[48,6,1,256]{3,0,2,1:T(8,128)(2,1)S(1)} %get-tuple-element.15), channel_id=1, source_target_pairs={{1,0},{2,1},{3,2},{4,3},{5,4},{6,5},{7,6},{8,7},{9,8},{10,9},{11,1... | collective-permute-start | bytes 442376 | tf_op jit(solution)/shard_map/ppermute | solution.py:32
  36.6 36.8 %copy-start.7 = (bf16[3,3,3,48,48]{4,3,2,1,0:T(8,128)(2,1)S(1)}, bf16[3,3,3,48,48]{4,3,2,1,0:T(8,128)(2,1)}, u32[]{:S(2)}) copy-start(bf16[3,3,3,48,48]{4,3,2,1,0:T(8,128)(2,1)} %param.9) | copy-start | bytes 373252
  73.4 136.9 %copy-start.5 = (f32[48]{0:T(128)S(1)}, f32[48]{0:T(128)}, u32[]{:S(2)}) copy-start(f32[48]{0:T(128)} %param.10) | copy-start | bytes 580
  215.7 2.3 copy-start.2
  219.6 12.0 %collective-permute-start.4 = (bf16[48,1,20,256]{3,0,2,1:T(8,128)(2,1)}, bf16[48,1,20,256]{3,0,2,1:T(8,128)(2,1)S(1)}, u32[]{:S(2)}, u32[]{:S(2)}) collective-permute-start(bf16[48,1,20,256]{3,0,2,1:T(8,128)(2,1)} %copy.41), channel_id=1, source_target_pairs={{0,32},{32,64},{64,96},{1,33},{33,65},{65,97},{2,34},{34,66},{66,9... | collective-permute-start | bytes 1474568 | tf_op jit(solution)/shard_map/ppermute | solution.py:31
  224.3 12.6 %collective-permute-start.5 = (bf16[48,1,20,256]{3,0,2,1:T(8,128)(2,1)}, bf16[48,1,20,256]{3,0,2,1:T(8,128)(2,1)S(1)}, u32[]{:S(2)}, u32[]{:S(2)}) collective-permute-start(bf16[48,1,20,256]{3,0,2,1:T(8,128)(2,1)} %copy.42), channel_id=1, source_target_pairs={{32,0},{64,32},{96,64},{33,1},{65,33},{97,65},{34,2},{66,34},{98,6... | collective-permute-start | bytes 1474568 | tf_op jit(solution)/shard_map/ppermute | solution.py:32
  230.3 14.5 %copy-start.4 = (s32[4,20,256]{2,0,1:T(4,128)S(1)}, s32[4,20,256]{2,0,1:T(4,128)}, u32[]{:S(2)}) copy-start(s32[4,20,256]{2,0,1:T(4,128)} %param.13) | copy-start | bytes 245764
  237.6 17.7 %collective-permute-start.6 = (bf16[48,6,1,256]{3,0,2,1:T(8,128)(2,1)}, bf16[48,6,1,256]{3,0,2,1:T(8,128)(2,1)S(1)}, u32[]{:S(2)}, u32[]{:S(2)}) collective-permute-start(bf16[48,6,1,256]{3,0,2,1:T(8,128)(2,1)} %get-tuple-element.12), channel_id=1, source_target_pairs={{0,1},{1,2},{2,3},{3,4},{4,5},{5,6},{6,7},{7,8},{8,9},{9,10},{10,1... | collective-permute-start | bytes 442376 | tf_op jit(solution)/shard_map/ppermute | solution.py:31
  242.8 12.6 %collective-permute-start.7 = (bf16[48,6,1,256]{3,0,2,1:T(8,128)(2,1)}, bf16[48,6,1,256]{3,0,2,1:T(8,128)(2,1)}, u32[]{:S(2)}, u32[]{:S(2)}) collective-permute-start(bf16[48,6,1,256]{3,0,2,1:T(8,128)(2,1)} %get-tuple-element.13), channel_id=1, source_target_pairs={{1,0},{2,1},{3,2},{4,3},{5,4},{6,5},{7,6},{8,7},{9,8},{10,9},{11,1... | collective-permute-start | bytes 442376 | tf_op jit(solution)/shard_map/ppermute | solution.py:32
  445.0 9.1 %copy-start.6 = (f32[64]{0:T(128)S(1)}, f32[64]{0:T(128)}, u32[]{:S(2)}) copy-start(f32[64]{0:T(128)} %param.12) | copy-start | bytes 772
  454.1 3.3 copy-start.1

commit v2 on v1

--- a/solution.py
+++ b/solution.py
@@ -16,34 +16,8 @@
 ROWS = BODY + 16
 DEVS = 128
 GROUPS = 160
+AHEAD = 4
 MESH = pl.DeviceIdType.MESH
-
-CONV_LAYOUT = ("NCDHW", "DHWOI", "NCDHW")
-
-
-def extended(array, sides, width):
-    for axis, dim in sides:
-        devices, length = (lax.axis_size(axis), array.shape[dim])
-        up = [(i, (i + 1) % devices) for i in range(devices - 1)]
-        down = [(j, i) for i, j in up]
-        last = lax.slice_in_dim(array, length - width, length, axis=dim)
-        leading = lax.slice_in_dim(array, 0, width, axis=dim)
-        before = lax.ppermute(last, axis, up)
-        after = lax.ppermute(leading, axis, down)
-        array = jnp.concatenate([before, array, after], axis=dim)
-    return array
-
-
-def convolve(padded, weight, bias):
-    summed = lax.conv_general_dilated(
-        padded[None],
-        weight,
-        (1, 1, 1),
-        ((0, 0), (0, 0), (1, 1)),
-        dimension_numbers=CONV_LAYOUT,
-        preferred_element_type=jnp.float32,
-    )[0]
-    return summed + bias[:, None, None, None]
 
 
 def table_kernel(blocks_ref, labels_ref, owner_ref, table_ref, held, scalars, used, sem):
@@ -102,6 +76,272 @@
     )(blocks, labels, owner_map)
 
 
+FEATURE_CHUNKS = ((0, 5), (5, 5), (10, 5), (15, 5))
+HIDDEN_CHUNKS = ((0, 4), (4, 5), (9, 5), (14, 6))
+LAST_CHUNKS = ((0, 3), (3, 5), (8, 5), (13, 7))
+PER_EXCHANGE = 14
+
+
+def halo_copies(own, side_z, side_y, chunks, base, send_sem, recv_sem):
+    gz, xy = lax.axis_index("gz"), lax.axis_index("xy")
+    depth, height = lax.axis_size("gz"), lax.axis_size("xy")
+    plan = []
+    for c, (first, length) in enumerate(chunks):
+        rows = pl.ds(first, length)
+        plan.append(((1, 0), own.at[3, rows], side_z.at[0, rows]))
+        plan.append(((-1, 0), own.at[0, rows], side_z.at[1, rows]))
+    plan.append(((0, 1), own.at[:, 19], side_y.at[0, pl.ds(1, 4)]))
+    plan.append(((0, -1), own.at[:, 0], side_y.at[1, pl.ds(1, 4)]))
+    plan.append(((1, 1), own.at[3, 19], side_y.at[0, 0]))
+    plan.append(((1, -1), own.at[3, 0], side_y.at[1, 0]))
+    plan.append(((-1, 1), own.at[0, 19], side_y.at[0, 5]))
+    plan.append(((-1, -1), own.at[0, 0], side_y.at[1, 5]))
+    copies = []
+    for i, ((dz, dy), src, dst) in enumerate(plan):
+        def inside(a, b):
+            return (a >= 0) & (a < depth) & (b >= 0) & (b < height)
+
+        copy = pltpu.make_async_remote_copy(
+            src_ref=src,
+            dst_ref=dst,
+            send_sem=send_sem.at[base + i],
+            recv_sem=recv_sem.at[base + i],
+            device_id=(gz + dz, xy + dy),
+            device_id_type=MESH,
+        )
+        copies.append((copy, inside(gz + dz, xy + dy), inside(gz - dz, xy - dy)))
+    return copies
+
+
+def start(entry):
+    @pl.when(entry[1])
+    def _():
+        entry[0].start()
+
+
+def arrive(entry):
+    @pl.when(entry[2])
+    def _():
+        entry[0].wait_recv()
+
+
+def leave(entry):
+    @pl.when(entry[1])
+    def _():
+        entry[0].wait_send()
+
+
+def conv_kernel(
+    own, w1, b1, w2, b2, emb_ref, wide, hwide, hidden, fz, fy, hz, hy, part1, part2,
+    send_sem, recv_sem,
+):
+    gz, xy = lax.axis_index("gz"), lax.axis_index("xy")
+    depth, height = lax.axis_size("gz"), lax.axis_size("xy")
+    barrier = pltpu.get_barrier_semaphore()
+    near = [(a, b) for a in (-1, 0, 1) for b in (-1, 0, 1) if (a, b) != (0, 0)]
+
+    def exists(a, b):
+        return (gz + a >= 0) & (gz + a < depth) & (xy + b >= 0) & (xy + b < height)
+
+    for a, b in near:
+        @pl.when(exists(a, b))
+        def _():
+            pl.semaphore_signal(
+                barrier, inc=1, device_id=(gz + a, xy + b), device_id_type=MESH
+            )
+
+    for side, has in ((0, gz == 0), (1, gz == depth - 1)):
+        @pl.when(has)
+        def _():
+            zeros = jnp.zeros(fz.shape[1:], fz.dtype)
+            fz[side] = zeros
+            hz[side] = zeros
+            for s in range(2):
+                fy[s, 5 * side] = jnp.zeros(fy.shape[2:], fy.dtype)
+                hy[s, 5 * side] = jnp.zeros(fy.shape[2:], fy.dtype)
+
+    for side, has in ((0, xy == 0), (1, xy == height - 1)):
+        @pl.when(has)
+        def _():
+            fy[side] = jnp.zeros(fy.shape[1:], fy.dtype)
+            hy[side] = jnp.zeros(fy.shape[1:], fy.dtype)
+
+    beside_z = jnp.where(gz > 0, 1, 0) + jnp.where(gz < depth - 1, 1, 0)
+    beside_y = jnp.where(xy > 0, 1, 0) + jnp.where(xy < height - 1, 1, 0)
+    pl.semaphore_wait(barrier, (1 + beside_z) * (1 + beside_y) - 1)
+
+    first = halo_copies(own, fz, fy, FEATURE_CHUNKS, 0, send_sem, recv_sem)
+    then = halo_copies(hidden, hz, hy, HIDDEN_CHUNKS, PER_EXCHANGE, send_sem, recv_sem)
+    for entry in first[8:] + first[:8]:
+        start(entry)
+
+    lane = lax.broadcasted_iota(jnp.int32, (48, 256), 1)
+
+    def put(ref, e, y, value):
+        turned = value.astype(jnp.float32)
+        left = jnp.where(lane == 0, 0.0, pltpu.roll(turned, 1, 1))
+        right = jnp.where(lane == 255, 0.0, pltpu.roll(turned, 255, 1))
+        ref[e, y, 0:48, :] = left.astype(jnp.bfloat16)
+        ref[e, y, 48:96, :] = value
+        ref[e, y, 96:144, :] = right.astype(jnp.bfloat16)
+
+    def slab(ref, e, y):
+        return ref[e, pl.ds(y, 3)].reshape(432, 256)
+
+    def product(w, ref, e, y, low, high, channels):
+        r = jnp.dot(
+            w[low * channels : (high + 1) * channels, :],
+            slab(ref, e, y),
+            preferred_element_type=jnp.float32,
+        )
+        return {
+            e - dz: r[(dz - low) * channels : (dz - low + 1) * channels]
+            for dz in range(low, high + 1)
+        }
+
+    def inner(w, ref, y, channels):
+        total = {}
+        for e, low, high in ((1, 0, 1), (2, 0, 2), (3, 0, 2), (4, 1, 2)):
+            for z, v in product(w, ref, e, y, low, high, channels).items():
+                total[z] = total[z] + v if z in total else v
+        return total
+
+    def fill(y, carry):
+        for z in range(4):
+            put(wide, z + 1, y + 1, own[z, y])
+        return carry
+
+    lax.fori_loop(0, 20, fill, 0)
+    for entry in first[8:]:
+        arrive(entry)
+
+    def fill_side(e, carry):
+        put(wide, e, 0, fy[0, e])
+        put(wide, e, 21, fy[1, e])
+        return carry
+
+    lax.fori_loop(0, 6, fill_side, 0)
+
+    bias1 = jnp.broadcast_to(b1[...], (48, 256))
+    bias2 = jnp.broadcast_to(b2[...], (64, 256))
+
+    def keep_hidden(z, y, total):
+        value = jnp.maximum(total + bias1, 0.0).astype(jnp.bfloat16)
+        hidden[z, y] = value
+        put(hwide, z + 1, y + 1, value)
+
+    def first_inner(y, carry):
+        total = inner(w1, wide, y, 48)
+        part1[0, y] = total[0]
+        part1[1, y] = total[3]
+        keep_hidden(1, y, total[1])
+        keep_hidden(2, y, total[2])
+        return carry
+
+    lax.fori_loop(0, 20, first_inner, 0, unroll=2)
+
+    def fill_z(y, carry):
+        put(wide, 0, y + 1, fz[0, y])
+        put(wide, 5, y + 1, fz[1, y])
+        return carry
+
+    def first_outer(y, carry):
+        keep_hidden(0, y, part1[0, y] + product(w1, wide, 0, y, 0, 0, 48)[0])
+        keep_hidden(3, y, part1[1, y] + product(w1, wide, 5, y, 2, 2, 48)[3])
+        return carry
+
+    for c in range(4):
+        arrive(first[2 * c])
+        arrive(first[2 * c + 1])
+        low, length = FEATURE_CHUNKS[c]
+        lax.fori_loop(low, low + length, fill_z, 0)
+        low, length = HIDDEN_CHUNKS[c]
+        lax.fori_loop(low, low + length, first_outer, 0)
+        start(then[2 * c])
+        start(then[2 * c + 1])
+        if c == 0:
+            for i in (9, 11, 13):
+                start(then[i])
+    for i in (8, 10, 12):
+        start(then[i])
+
+    for entry in then[8:]:
+        arrive(entry)
+
+    def hidden_side(e, carry):
+        put(hwide, e, 0, hy[0, e])
+        put(hwide, e, 21, hy[1, e])
+        return carry
+
+    lax.fori_loop(0, 6, hidden_side, 0)
+
+    def keep(z, y, total):
+        value = (total + bias2).astype(jnp.bfloat16)
+        group = (z * 20 + y) * 2
+        emb_ref[group] = value[:, 0:128]
+        emb_ref[group + 1] = value[:, 128:256]
+
+    def second_inner(y, carry):
+        total = inner(w2, hwide, y, 64)
+        part2[0, y] = total[0]
+        part2[1, y] = total[3]
+        keep(1, y, total[1])
+        keep(2, y, total[2])
+        return carry
+
+    lax.fori_loop(0, 20, second_inner, 0, unroll=2)
+
+    def hidden_z(y, carry):
+        put(hwide, 0, y + 1, hz[0, y])
+        put(hwide, 5, y + 1, hz[1, y])
+        return carry
+
+    def second_outer(y, carry):
+        keep(0, y, part2[0, y] + product(w2, hwide, 0, y, 0, 0, 64)[0])
+        keep(3, y, part2[1, y] + product(w2, hwide, 5, y, 2, 2, 64)[3])
+        return carry
+
+    for c in range(4):
+        arrive(then[2 * c])
+        arrive(then[2 * c + 1])
+        low, length = HIDDEN_CHUNKS[c]
+        lax.fori_loop(low, low + length, hidden_z, 0)
+        low, length = LAST_CHUNKS[c]
+        lax.fori_loop(low, low + length, second_outer, 0)
+
+    for entry in first + then:
+        leave(entry)
+
+
+def embed(features, first_weight, first_bias, second_weight, second_bias):
+    own = features.transpose(1, 2, 0, 3)
+    w1 = first_weight.transpose(0, 3, 1, 2, 4).reshape(144, 432)
+    w2 = second_weight.transpose(0, 3, 1, 2, 4).reshape(192, 432)
+    bf, f32 = jnp.bfloat16, jnp.float32
+    return pl.pallas_call(
+        conv_kernel,
+        out_shape=jax.ShapeDtypeStruct((GROUPS, EMB, 128), bf),
+        in_specs=[pl.BlockSpec(memory_space=pltpu.VMEM)] * 5,
+        out_specs=pl.BlockSpec(memory_space=pltpu.VMEM),
+        scratch_shapes=[
+            pltpu.VMEM((6, 22, 144, 256), bf),
+            pltpu.VMEM((6, 22, 144, 256), bf),
+            pltpu.VMEM((4, 20, 48, 256), bf),
+            pltpu.VMEM((2, 20, 48, 256), bf),
+            pltpu.VMEM((2, 6, 48, 256), bf),
+            pltpu.VMEM((2, 20, 48, 256), bf),
+            pltpu.VMEM((2, 6, 48, 256), bf),
+            pltpu.VMEM((2, 20, 48, 256), f32),
+            pltpu.VMEM((2, 20, 64, 256), f32),
+            pltpu.SemaphoreType.DMA((2 * PER_EXCHANGE,)),
+            pltpu.SemaphoreType.DMA((2 * PER_EXCHANGE,)),
+        ],
+        compiler_params=pltpu.CompilerParams(
+            collective_id=1, has_side_effects=True, vmem_limit_bytes=52 << 20
+        ),
+    )(own, w1, first_bias[:, None], w2, second_bias[:, None])
+
+
 def place(device):
     return (device // 32, lax.rem(device, 32))
 
@@ -122,11 +362,11 @@
     upper = (inner >= HALF) | (inner >= outer)
     diagonal = inner == outer
     line = lax.broadcasted_iota(jnp.int32, (16, 128), 0)
-    zero = jnp.zeros((EMB, 256), jnp.bfloat16)
     one = jnp.ones((EMB, 256), jnp.bfloat16)
+    near = lax.broadcasted_iota(jnp.int32, (EMB, 128), 1) < EMB
     extras = jnp.zeros((16, 128), jnp.float32)
     for p in range(PAIRS):
-        lefts, rights, masks, sizes, rows = [], [], [], [], []
+        parts, sizes, rows = [], [], []
         for h in range(2):
             code = table_ref[device * SLOTS + 2 * p + h]
             start = code >> 15
@@ -139,27 +379,18 @@
             second = emb_ref[jnp.minimum(group + 1, GROUPS - 1)]
             in_first = jnp.where((lane >= low) & (lane < low + size), 1.0, 0.0).astype(jnp.bfloat16)
             in_second = jnp.where(lane + 128 < low + size, 1.0, 0.0).astype(jnp.bfloat16)
-            lefts += [first * in_first, second * in_second]
-            masks += [in_first, in_second]
-            rights.append(jnp.concatenate([first, second], axis=1))
-        mask_rows = jnp.broadcast_to(jnp.concatenate(masks, axis=1), (16, 512))
-        left = jnp.concatenate([jnp.concatenate(lefts, axis=1), mask_rows], axis=0)
-        right = jnp.concatenate(
-            [
-                jnp.concatenate([rights[0], zero], axis=1),
-                jnp.concatenate([zero, rights[1]], axis=1),
-                jnp.concatenate([one, zero], axis=1),
-                jnp.concatenate([zero, one], axis=1),
-            ],
-            axis=0,
-        )
-        result = lax.dot_general(
-            left, right, (((1,), (1,)), ((), ())), preferred_element_type=jnp.float32
-        )
+            mask_rows = jnp.broadcast_to(jnp.concatenate([in_first, in_second], axis=1), (16, 256))
+            whole = jnp.concatenate([first, second], axis=1)
+            left = jnp.concatenate([jnp.concatenate([first * in_first, second * in_second], axis=1), mask_rows], axis=0)
+            right = jnp.concatenate([whole, one] if h == 0 else [one, whole], axis=0)
+            parts.append(lax.dot_general(left, right, (((1,), (1,)), ((), ())), preferred_element_type=jnp.float32))
         size_row = jnp.where(lane < EMB, sizes[0], sizes[1])
         owner_row = jnp.where(lane < EMB, rows[0], rows[1])
-        mean = result[EMB : EMB + 1, 0:128] / jnp.maximum(size_row, 1.0)
-        centred = result[0:EMB, 0:128] - result[0:EMB, 128:256] * mean
+        second_row = jnp.where(near[0:1], parts[0][EMB : EMB + 1], parts[1][EMB : EMB + 1])
+        mean = second_row / jnp.maximum(size_row, 1.0)
+        square = jnp.where(near, parts[0][0:EMB], parts[1][0:EMB])
+        column = pltpu.roll(jnp.where(near, parts[1][0:EMB], parts[0][0:EMB]), EMB, 1)
+        centred = square - column * mean
         rolled = pltpu.roll(centred[HALF:EMB], 96, 1)
         packed = jnp.where(upper, centred[0:HALF], rolled)
         send_ref[device, p * HALF : (p + 1) * HALF, :] = packed.astype(jnp.bfloat16)
@@ -187,7 +418,8 @@
         return carry
 
     lax.fori_loop(1, DEVS, greet, 0)
-    moments_of(emb_ref, table_ref, me, send_ref)
+    for k in range(AHEAD):
+        moments_of(emb_ref, table_ref, partner(me, k), send_ref)
     own = pltpu.make_async_copy(send_ref.at[me], got_ref.at[me], own_sem)
     own.start()
     pl.semaphore_wait(barrier, DEVS - 1)
@@ -203,12 +435,17 @@
             device_id_type=MESH,
         )
 
-    def send(k, carry):
-        moments_of(emb_ref, table_ref, partner(me, k), send_ref)
+    for k in range(1, AHEAD):
         copy(k).start()
-        return carry
-
-    lax.fori_loop(1, DEVS, send, 0)
+
+    def send(i, carry):
+        for t in range(AHEAD):
+            moments_of(emb_ref, table_ref, partner(me, i * AHEAD + t), send_ref)
+        for t in range(AHEAD):
+            copy(i * AHEAD + t).start()
+        return carry
+
+    lax.fori_loop(1, DEVS // AHEAD, send, 0)
 
     def finish(k, carry):
         copy(k).wait()
@@ -426,11 +663,7 @@
     features, first_weight, first_bias, second_weight, second_bias, labels, blocks, owner_map
 ):
     table = slot_table(blocks.reshape(blocks.shape[2], blocks.shape[3]), labels, owner_map)
-    padded = extended(features, (("gz", 1), ("xy", 2)), 1)
-    hidden = jax.nn.relu(convolve(padded, first_weight, first_bias)).astype(jnp.bfloat16)
-    hidden_pad = extended(hidden, (("gz", 1), ("xy", 2)), 1)
-    embedding = convolve(hidden_pad, second_weight, second_bias).astype(jnp.bfloat16)
-    grouped = embedding.reshape(EMB, GROUPS, 128).transpose(1, 0, 2)
+    grouped = embed(features, first_weight, first_bias, second_weight, second_bias)
     return totals(exchange(grouped, table))
 
 

time: 569 us -> 149 us (0.26); the launches traced: 560 us -> 148 us
  matrix products: 287 us -> 0 us
  local copies, waits for them, and re-layouts: 98.8 us -> 9.59 us
  Pallas kernels: 111 us -> 138 us
  starting transfers between devices: 24.1 us -> 0 us
  waiting for transfers between devices: 23.1 us -> 0 us
  other arithmetic: 14.5 us -> 0 us
    conv_general_dilated x2 -> x0, matrix products: 287 us -> none  [convolve(): lax.conv_general_dilated(padded[None], weight, (1, 1, 1), ((0, 0), (0, 0)...]
    broadcast_in_dim x2, local copies, waits for them, and re-layouts: 73.5 us -> 1.63 us  [the longest x1 0.89 us: embed(): first_bias[:, None]]
    pallas_call x0 -> x1, Pallas kernels: none -> 44.1 us  [embed(): pl.pallas_call(conv_kernel, out_shape=jax.ShapeDtypeStruct((GROUPS, EMB,...]
    ppermute x8 -> x0, starting transfers between devices: 24.1 us -> none  [the longest x4 17.7 us: extended(): before = lax.ppermute(last, axis, up)]
    ppermute x8 -> x0, waiting for transfers between devices: 23.1 us -> none  [the longest x4 13.2 us: extended(): after = lax.ppermute(leading, axis, down)]
    pallas_call x1, Pallas kernels: 80.5 us -> 62.8 us  [exchange(): pl.pallas_call(exchange_kernel, out_shape=jax.ShapeDtypeStruct((DEVS, ROW...]
    squeeze x1 -> x0, local copies, waits for them, and re-layouts: 9.08 us -> none  [convolve(): lax.conv_general_dilated(padded[None], weight, (1, 1, 1), ((0, 0), (0, 0)...]
    slice x5 -> x0, local copies, waits for them, and re-layouts: 6.72 us -> none  [the longest x2 5.14 us: extended(): leading = lax.slice_in_dim(array, 0, width, axis=dim)]
  transfers between devices with their start and end apart: 8 -> 0, of which waited for: 6 -> 0; matrix products, arithmetic and copies ran while one was open for 1% -> 0% of each run, Pallas kernels for 2% -> 0%
where the time goes in v2:
time: 149 us; the launch traced here: 148 us
  Pallas kernels  138 us (93%)
  local copies, waits for them, and re-layouts  9.59 us (6%)
    pallas_call x1, Pallas kernels, exchange(): pl.pallas_call(exchange_kernel, out_shape=jax.ShapeDtypeStruct((DEVS, ROW...  62.8 us
    pallas_call x1, Pallas kernels, embed(): pl.pallas_call(conv_kernel, out_shape=jax.ShapeDtypeStruct((GROUPS, EMB,...  44.1 us
    pallas_call x1, Pallas kernels, totals(): pl.pallas_call(total_kernel, out_shape=(jax.ShapeDtypeStruct((SV_DEV, EMB...  21 us
    pallas_call x1, Pallas kernels, slot_table(): pl.pallas_call(table_kernel, out_shape=jax.ShapeDtypeStruct((DEVS * SLOTS...  9.94 us
    unnamed x10, local copies, waits for them, and re-layouts  5.23 us

profile of v2, /device:TPU:1, one launch (start us, length us, event | category | flops | bytes accessed | tf_op | source)
XLA Modules:
  0.0 148.1 jit_solution(6208026919522345120)
XLA Ops:
  0.6 0.0 copy-start.3
  0.6 0.0 copy-start.2
  0.6 0.9 copy.20.b1
  1.5 0.7 copy.22.b2
  2.3 1.5 %copy.23.labels_ref = s32[4,20,256]{2,1,0:T(8,128)} copy(s32[4,20,256]{2,0,1:T(4,128)} %param.13) | data formatting | bytes 163840 | tf_op args[5]
  3.8 9.9 %shard_map.96.table_ref = s32[768]{0:T(1024)} custom-call(s32[256,128]{1,0:T(8,128)} %bitcast.11, s32[4,20,256]{2,1,0:T(8,128)} %copy.23.labels_ref, s32[16384]{0:T(1024)} %owner_ref.1), custom_call_target="tpu_custom_call" | custom-call | tf_op jit(solution)/shard_map/pallas_call | solution.py:61
  13.8 1.1 copy.18
  14.9 0.3 reshape.13.w1
  15.2 0.0 copy-done.3
  15.2 0.3 copy.25
  15.5 0.3 reshape.16.w2
  15.8 0.0 copy-done.2
  15.9 1.9 %copy.28 = bf16[48,4,20,256]{3,0,2,1:T(8,128)(2,1)} copy(bf16[48,4,20,256]{3,1,2,0:T(4,128)(2,1)S(1)} %copy-done.2) | data formatting | bytes 3932160 | tf_op args[0]
  17.8 0.0 copy-start.1
  17.8 44.1 %shard_map.95.emb_ref = bf16[160,64,128]{2,1,0:T(8,128)(2,1)} custom-call(bf16[4,20,48,256]{3,2,1,0:T(8,128)(2,1)} %bitcast.8, bf16[144,432]{1,0:T(8,128)(2,1)S(1)} %reshape.13.w1, f32[48,1]{1,0:T(8,128)S(1)} %copy.20.b1, bf16[192,432]{1,0:T(8,128)(2,1)S(1)} %reshape.16.w2, f32[64,1]{1,0:T(8,128)S(1)} %copy.22.b2), custom_call_target="tpu_custom_call" | custom-call | tf_op jit(solution)/shard_map/pallas_call | solution.py:321
  61.9 0.0 copy-done.1
  61.9 0.0 copy-start
  61.9 1.7 %copy-done = bf16[160,64,128]{2,1,0:T(8,128)(2,1)S(1)} copy-done((bf16[160,64,128]{2,1,0:T(8,128)(2,1)S(1)}, bf16[160,64,128]{2,1,0:T(8,128)(2,1)}, u32[]{:S(2)}) %copy-start) | copy-done | bytes 2621464
  63.7 62.8 %shard_map.97.got_ref = bf16[128,112,128]{2,1,0:T(8,128)(2,1)S(1)} custom-call(bf16[160,64,128]{2,1,0:T(8,128)(2,1)S(1)} %copy-done, s32[768]{0:T(1024)S(1)} %copy-done.1), custom_call_target="tpu_custom_call" | custom-call | tf_op jit(solution)/shard_map/pallas_call | solution.py:459
  126.5 21.0 %shard_map.98 = (f32[128,64]{1,0:T(8,128)S(1)}, f32[128,4096]{1,0:T(8,128)}) custom-call(bf16[128,112,128]{2,1,0:T(8,128)(2,1)S(1)} %shard_map.97.got_ref), custom_call_target="tpu_custom_call" | custom-call | tf_op jit(solution)/shard_map/pallas_call | solution.py:631
  147.4 0.7 copy.24
Async XLA Ops:
  0.6 14.6 %copy-start.3 = (bf16[3,3,3,64,48]{3,4,2,1,0:T(8,128)(2,1)S(1)}, bf16[3,3,3,64,48]{3,4,2,1,0:T(8,128)(2,1)}, u32[]{:S(2)}) copy-start(bf16[3,3,3,64,48]{3,4,2,1,0:T(8,128)(2,1)} %param.11) | copy-start | bytes 497668
  0.6 15.2 %copy-start.2 = (bf16[48,4,20,256]{3,1,2,0:T(4,128)(2,1)S(1)}, bf16[48,4,20,256]{3,1,2,0:T(4,128)(2,1)}, u32[]{:S(2)}) copy-start(bf16[48,4,20,256]{3,1,2,0:T(4,128)(2,1)} %param.8) | copy-start | bytes 5898244
  17.8 44.1 %copy-start.1 = (s32[768]{0:T(1024)S(1)}, s32[768]{0:T(1024)}, u32[]{:S(2)}) copy-start(s32[768]{0:T(1024)} %shard_map.96.table_ref) | copy-start | bytes 9220
  61.9 1.7 %copy-start = (bf16[160,64,128]{2,1,0:T(8,128)(2,1)S(1)}, bf16[160,64,128]{2,1,0:T(8,128)(2,1)}, u32[]{:S(2)}) copy-start(bf16[160,64,128]{2,1,0:T(8,128)(2,1)} %shard_map.95.emb_ref) | copy-start | bytes 7864324

commit v3 on v2

--- a/solution.py
+++ b/solution.py
@@ -18,62 +18,6 @@
 GROUPS = 160
 AHEAD = 4
 MESH = pl.DeviceIdType.MESH
-
-
-def table_kernel(blocks_ref, labels_ref, owner_ref, table_ref, held, scalars, used, sem):
-    lists = blocks_ref[...]
-    sizes = jnp.sum(jnp.where(lists >= 0, 1, 0), axis=1, keepdims=True)
-    lane = lax.broadcasted_iota(jnp.int32, lists.shape, 1)
-    both = jnp.where(lane == 0, lists, sizes).astype(jnp.float32)
-    held[...] = both.T[0:8, :].astype(jnp.int32)
-    copy = pltpu.make_async_copy(held, scalars, sem)
-    copy.start()
-
-    def clear_used(d, carry):
-        used[d] = 0
-        return carry
-
-    def clear_table(d, carry):
-        table_ref[d] = 0
-        return carry
-
-    lax.fori_loop(0, DEVS, clear_used, 0, unroll=8)
-    lax.fori_loop(0, DEVS * SLOTS, clear_table, 0, unroll=8)
-    copy.wait()
-
-    def step(b, carry):
-        start = scalars[0, b]
-        size = scalars[1, b]
-        line = start >> 8
-        z = line // 20
-        row = owner_ref[labels_ref[z, line - z * 20, start & 255]]
-        device = row >> 7
-        rank = used[device]
-        used[device] = rank + 1
-        table_ref[device * SLOTS + rank] = (start << 15) + (size << 7) + (row & 127)
-        return carry
-
-    lax.fori_loop(0, lists.shape[0], step, 0, unroll=4)
-
-
-def slot_table(blocks, labels, owner_map):
-    count = blocks.shape[0]
-    return pl.pallas_call(
-        table_kernel,
-        out_shape=jax.ShapeDtypeStruct((DEVS * SLOTS,), jnp.int32),
-        in_specs=[
-            pl.BlockSpec(memory_space=pltpu.VMEM),
-            pl.BlockSpec(memory_space=pltpu.SMEM),
-            pl.BlockSpec(memory_space=pltpu.SMEM),
-        ],
-        out_specs=pl.BlockSpec(memory_space=pltpu.SMEM),
-        scratch_shapes=[
-            pltpu.VMEM((8, count), jnp.int32),
-            pltpu.SMEM((8, count), jnp.int32),
-            pltpu.SMEM((DEVS,), jnp.int32),
-            pltpu.SemaphoreType.DMA,
-        ],
-    )(blocks, labels, owner_map)
 
 
 FEATURE_CHUNKS = ((0, 5), (5, 5), (10, 5), (15, 5))
@@ -131,24 +75,19 @@
         entry[0].wait_send()
 
 
-def conv_kernel(
-    own, w1, b1, w2, b2, emb_ref, wide, hwide, hidden, fz, fy, hz, hy, part1, part2,
-    send_sem, recv_sem,
+def main_kernel(
+    own, w1, b1, w2, b2, lists_ref, labels_hbm, owner_hbm, got_ref, wide, hwide, hidden,
+    fz, fy, hz, hy, part1, part2, emb_ref, send_ref, labels_ref, owner_ref, facts, scalars,
+    rows_s, rows_v, table_v, table_ref, send_sem, recv_sem, far_send, far_recv, own_sem, here_sem,
 ):
     gz, xy = lax.axis_index("gz"), lax.axis_index("xy")
     depth, height = lax.axis_size("gz"), lax.axis_size("xy")
+    me = gz * 32 + xy
     barrier = pltpu.get_barrier_semaphore()
-    near = [(a, b) for a in (-1, 0, 1) for b in (-1, 0, 1) if (a, b) != (0, 0)]
-
-    def exists(a, b):
-        return (gz + a >= 0) & (gz + a < depth) & (xy + b >= 0) & (xy + b < height)
-
-    for a, b in near:
-        @pl.when(exists(a, b))
-        def _():
-            pl.semaphore_signal(
-                barrier, inc=1, device_id=(gz + a, xy + b), device_id_type=MESH
-            )
+    labels_copy = pltpu.make_async_copy(labels_hbm, labels_ref, here_sem.at[0])
+    owner_copy = pltpu.make_async_copy(owner_hbm, owner_ref, here_sem.at[1])
+    labels_copy.start()
+    owner_copy.start()
 
     for side, has in ((0, gz == 0), (1, gz == depth - 1)):
         @pl.when(has)
@@ -166,15 +105,6 @@
             fy[side] = jnp.zeros(fy.shape[1:], fy.dtype)
             hy[side] = jnp.zeros(fy.shape[1:], fy.dtype)
 
-    beside_z = jnp.where(gz > 0, 1, 0) + jnp.where(gz < depth - 1, 1, 0)
-    beside_y = jnp.where(xy > 0, 1, 0) + jnp.where(xy < height - 1, 1, 0)
-    pl.semaphore_wait(barrier, (1 + beside_z) * (1 + beside_y) - 1)
-
-    first = halo_copies(own, fz, fy, FEATURE_CHUNKS, 0, send_sem, recv_sem)
-    then = halo_copies(hidden, hz, hy, HIDDEN_CHUNKS, PER_EXCHANGE, send_sem, recv_sem)
-    for entry in first[8:] + first[:8]:
-        start(entry)
-
     lane = lax.broadcasted_iota(jnp.int32, (48, 256), 1)
 
     def put(ref, e, y, value):
@@ -184,6 +114,35 @@
         ref[e, y, 0:48, :] = left.astype(jnp.bfloat16)
         ref[e, y, 48:96, :] = value
         ref[e, y, 96:144, :] = right.astype(jnp.bfloat16)
+
+    def greet(k):
+        pl.semaphore_signal(
+            barrier, inc=1, device_id=place(partner(me, k)), device_id_type=MESH
+        )
+
+    def fill(y, carry):
+        for k in range(6):
+            greet(1 + y * 6 + k)
+        for z in range(4):
+            put(wide, z + 1, y + 1, own[z, y])
+        return carry
+
+    lax.fori_loop(0, 20, fill, 0)
+    for k in range(121, DEVS):
+        greet(k)
+    count = lists_ref.shape[0]
+    lists = lists_ref[...]
+    sizes = jnp.sum(jnp.where(lists >= 0, 1, 0), axis=1, keepdims=True)
+    column = lax.broadcasted_iota(jnp.int32, lists.shape, 1)
+    facts[...] = jnp.where(column == 0, lists, sizes).astype(jnp.float32).T[0:8, :].astype(jnp.int32)
+    facts_copy = pltpu.make_async_copy(facts, scalars, here_sem.at[2])
+    facts_copy.start()
+    pl.semaphore_wait(barrier, DEVS - 1)
+
+    first = halo_copies(own, fz, fy, FEATURE_CHUNKS, 0, send_sem, recv_sem)
+    then = halo_copies(hidden, hz, hy, HIDDEN_CHUNKS, PER_EXCHANGE, send_sem, recv_sem)
+    for entry in first[8:] + first[:8]:
+        start(entry)
 
     def slab(ref, e, y):
         return ref[e, pl.ds(y, 3)].reshape(432, 256)
@@ -206,12 +165,6 @@
                 total[z] = total[z] + v if z in total else v
         return total
 
-    def fill(y, carry):
-        for z in range(4):
-            put(wide, z + 1, y + 1, own[z, y])
-        return carry
-
-    lax.fori_loop(0, 20, fill, 0)
     for entry in first[8:]:
         arrive(entry)
 
@@ -239,6 +192,47 @@
         return carry
 
     lax.fori_loop(0, 20, first_inner, 0, unroll=2)
+
+    labels_copy.wait()
+    owner_copy.wait()
+    facts_copy.wait()
+
+    def look(b, carry):
+        at = scalars[0, b]
+        run = at >> 8
+        z = jnp.clip((run * 3277) >> 16, 0, 3)
+        label = labels_ref[z, jnp.clip(run - z * 20, 0, 19), at & 255]
+        rows_s[0, b] = owner_ref[label & (owner_ref.shape[0] - 1)]
+        return carry
+
+    lax.fori_loop(0, count, look, 0, unroll=8)
+    rows_copy = pltpu.make_async_copy(rows_s, rows_v, here_sem.at[3])
+    rows_copy.start()
+    rows_copy.wait()
+    line8 = lax.broadcasted_iota(jnp.int32, (8, count), 0)
+    three = jnp.where(line8 == 2, jnp.broadcast_to(rows_v[0:1, :], (8, count)), facts[...])
+    turned3 = jnp.concatenate(
+        [three.astype(jnp.float32), jnp.zeros((120, count), jnp.float32)], axis=0
+    ).T.astype(jnp.int32)
+    row_of = turned3[:, 2:3]
+    code = (turned3[:, 0:1] << 15) + (turned3[:, 1:2] << 7) + (row_of & 127)
+    hit = (row_of >> 7) == lax.broadcasted_iota(jnp.int32, (count, DEVS), 1)
+    before = lax.broadcasted_iota(jnp.int32, (count, count), 0) > lax.broadcasted_iota(
+        jnp.int32, (count, count), 1
+    )
+    rank = jnp.dot(
+        jnp.where(before, 1.0, 0.0).astype(jnp.bfloat16),
+        jnp.where(hit, 1.0, 0.0).astype(jnp.bfloat16),
+        preferred_element_type=jnp.float32,
+    )
+    rank = jnp.where(hit, rank, -1.0)
+    slots = [
+        jnp.sum(jnp.where(rank == float(k), code, 0), axis=0, keepdims=True)
+        for k in range(SLOTS)
+    ]
+    table_v[...] = jnp.concatenate(slots + [slots[0], slots[0]], axis=0)
+    table_copy = pltpu.make_async_copy(table_v, table_ref, here_sem.at[4])
+    table_copy.start()
 
     def fill_z(y, carry):
         put(wide, 0, y + 1, fz[0, y])
@@ -309,20 +303,57 @@
         low, length = LAST_CHUNKS[c]
         lax.fori_loop(low, low + length, second_outer, 0)
 
+    table_copy.wait()
+
+    def copy(k):
+        device = partner(me, k)
+        return pltpu.make_async_remote_copy(
+            src_ref=send_ref.at[device],
+            dst_ref=got_ref.at[me],
+            send_sem=far_send.at[k],
+            recv_sem=far_recv.at[k],
+            device_id=place(device),
+            device_id_type=MESH,
+        )
+
+    for k in range(AHEAD):
+        moments_of(emb_ref, table_ref, partner(me, k), send_ref)
+    own_copy = pltpu.make_async_copy(send_ref.at[me], got_ref.at[me], own_sem)
+    own_copy.start()
+    for k in range(1, AHEAD):
+        copy(k).start()
+
+    def send(i, carry):
+        for t in range(AHEAD):
+            moments_of(emb_ref, table_ref, partner(me, i * AHEAD + t), send_ref)
+        for t in range(AHEAD):
+            copy(i * AHEAD + t).start()
+        return carry
+
+    lax.fori_loop(1, DEVS // AHEAD, send, 0)
     for entry in first + then:
         leave(entry)
 
-
-def embed(features, first_weight, first_bias, second_weight, second_bias):
+    def finish(k, carry):
+        copy(k).wait()
+        return carry
+
+    lax.fori_loop(1, DEVS, finish, 0)
+    own_copy.wait()
+
+
+def main(features, first_weight, first_bias, second_weight, second_bias, labels, blocks, owner_map):
     own = features.transpose(1, 2, 0, 3)
     w1 = first_weight.transpose(0, 3, 1, 2, 4).reshape(144, 432)
     w2 = second_weight.transpose(0, 3, 1, 2, 4).reshape(192, 432)
-    bf, f32 = jnp.bfloat16, jnp.float32
+    bf, f32, i32 = jnp.bfloat16, jnp.float32, jnp.int32
+    count = blocks.shape[0]
     return pl.pallas_call(
-        conv_kernel,
-        out_shape=jax.ShapeDtypeStruct((GROUPS, EMB, 128), bf),
-        in_specs=[pl.BlockSpec(memory_space=pltpu.VMEM)] * 5,
-        out_specs=pl.BlockSpec(memory_space=pltpu.VMEM),
+        main_kernel,
+        out_shape=jax.ShapeDtypeStruct((DEVS, ROWS, 128), bf),
+        in_specs=[pl.BlockSpec(memory_space=pltpu.VMEM)] * 6
+        + [pl.BlockSpec(memory_space=pl.ANY)] * 2,
+        out_specs=pl.BlockSpec(memory_space=pl.ANY),
         scratch_shapes=[
             pltpu.VMEM((6, 22, 144, 256), bf),
             pltpu.VMEM((6, 22, 144, 256), bf),
@@ -333,13 +364,27 @@
             pltpu.VMEM((2, 6, 48, 256), bf),
             pltpu.VMEM((2, 20, 48, 256), f32),
             pltpu.VMEM((2, 20, 64, 256), f32),
+            pltpu.VMEM((GROUPS, EMB, 128), bf),
+            pltpu.VMEM((DEVS, ROWS, 128), bf),
+            pltpu.SMEM(labels.shape, i32),
+            pltpu.SMEM(owner_map.shape, i32),
+            pltpu.VMEM((8, count), i32),
+            pltpu.SMEM((8, count), i32),
+            pltpu.SMEM((8, count), i32),
+            pltpu.VMEM((8, count), i32),
+            pltpu.VMEM((8, DEVS), i32),
+            pltpu.SMEM((8, DEVS), i32),
             pltpu.SemaphoreType.DMA((2 * PER_EXCHANGE,)),
             pltpu.SemaphoreType.DMA((2 * PER_EXCHANGE,)),
+            pltpu.SemaphoreType.DMA((DEVS,)),
+            pltpu.SemaphoreType.DMA((DEVS,)),
+            pltpu.SemaphoreType.DMA,
+            pltpu.SemaphoreType.DMA((5,)),
         ],
         compiler_params=pltpu.CompilerParams(
-            collective_id=1, has_side_effects=True, vmem_limit_bytes=52 << 20
+            collective_id=0, has_side_effects=True, vmem_limit_bytes=52 << 20
         ),
-    )(own, w1, first_bias[:, None], w2, second_bias[:, None])
+    )(own, w1, first_bias[:, None], w2, second_bias[:, None], blocks, labels, owner_map)
 
 
 def place(device):
@@ -368,12 +413,12 @@
     for p in range(PAIRS):
         parts, sizes, rows = [], [], []
         for h in range(2):
-            code = table_ref[device * SLOTS + 2 * p + h]
+            code = table_ref[2 * p + h, device]
             start = code >> 15
             size = (code >> 7) & 255
             rows.append((code & 127).astype(jnp.float32))
             sizes.append(size.astype(jnp.float32))
-            group = start >> 7
+            group = jnp.clip(start >> 7, 0, GROUPS - 1)
             low = start & 127
             first = emb_ref[group]
             second = emb_ref[jnp.minimum(group + 1, GROUPS - 1)]
@@ -407,75 +452,6 @@
     send_ref[device, BODY:ROWS, :] = extras.astype(jnp.bfloat16)
 
 
-def exchange_kernel(emb_ref, table_ref, got_ref, send_ref, send_sem, recv_sem, own_sem):
-    me = lax.axis_index("gz") * 32 + lax.axis_index("xy")
-    barrier = pltpu.get_barrier_semaphore()
-
-    def greet(k, carry):
-        pl.semaphore_signal(
-            barrier, inc=1, device_id=place(partner(me, k)), device_id_type=MESH
-        )
-        return carry
-
-    lax.fori_loop(1, DEVS, greet, 0)
-    for k in range(AHEAD):
-        moments_of(emb_ref, table_ref, partner(me, k), send_ref)
-    own = pltpu.make_async_copy(send_ref.at[me], got_ref.at[me], own_sem)
-    own.start()
-    pl.semaphore_wait(barrier, DEVS - 1)
-
-    def copy(k):
-        device = partner(me, k)
-        return pltpu.make_async_remote_copy(
-            src_ref=send_ref.at[device],
-            dst_ref=got_ref.at[me],
-            send_sem=send_sem.at[k],
-            recv_sem=recv_sem.at[k],
-            device_id=place(device),
-            device_id_type=MESH,
-        )
-
-    for k in range(1, AHEAD):
-        copy(k).start()
-
-    def send(i, carry):
-        for t in range(AHEAD):
-            moments_of(emb_ref, table_ref, partner(me, i * AHEAD + t), send_ref)
-        for t in range(AHEAD):
-            copy(i * AHEAD + t).start()
-        return carry
-
-    lax.fori_loop(1, DEVS // AHEAD, send, 0)
-
-    def finish(k, carry):
-        copy(k).wait()
-        return carry
-
-    lax.fori_loop(1, DEVS, finish, 0)
-    own.wait()
-
-
-def exchange(embedding, table):
-    return pl.pallas_call(
-        exchange_kernel,
-        out_shape=jax.ShapeDtypeStruct((DEVS, ROWS, 128), jnp.bfloat16),
-        in_specs=[
-            pl.BlockSpec(memory_space=pltpu.VMEM),
-            pl.BlockSpec(memory_space=pltpu.SMEM),
-        ],
-        out_specs=pl.BlockSpec(memory_space=pl.ANY),
-        scratch_shapes=[
-            pltpu.VMEM((DEVS, ROWS, 128), jnp.bfloat16),
-            pltpu.SemaphoreType.DMA((DEVS,)),
-            pltpu.SemaphoreType.DMA((DEVS,)),
-            pltpu.SemaphoreType.DMA,
-        ],
-        compiler_params=pltpu.CompilerParams(
-            collective_id=0, has_side_effects=True, vmem_limit_bytes=40 << 20
-        ),
-    )(embedding, table)
-
-
 CHUNKS = 4
 QUAD = 4
 
@@ -662,9 +638,17 @@
 def local(
     features, first_weight, first_bias, second_weight, second_bias, labels, blocks, owner_map
 ):
-    table = slot_table(blocks.reshape(blocks.shape[2], blocks.shape[3]), labels, owner_map)
-    grouped = embed(features, first_weight, first_bias, second_weight, second_bias)
-    return totals(exchange(grouped, table))
+    got = main(
+        features,
+        first_weight,
+        first_bias,
+        second_weight,
+        second_bias,
+        labels,
+        blocks.reshape(blocks.shape[2], blocks.shape[3]),
+        owner_map,
+    )
+    return totals(got)
 
 
 def solution(mesh):

time: 149 us -> 138 us (0.926)
  Pallas kernels: 138 us -> 126 us
    pallas_call x3 -> x1, Pallas kernels: 117 us -> 105 us  [main(): pl.pallas_call(main_kernel, out_shape=jax.ShapeDtypeStruct((DEVS, ROWS, 1...]
where the time goes in v3:
time: 138 us; the launch traced here: 137 us
  Pallas kernels  126 us (91%)
  local copies, waits for them, and re-layouts  10.2 us (7%)
    pallas_call x1, Pallas kernels, main(): pl.pallas_call(main_kernel, out_shape=jax.ShapeDtypeStruct((DEVS, ROWS, 1...  105 us
    pallas_call x1, Pallas kernels, totals(): pl.pallas_call(total_kernel, out_shape=(jax.ShapeDtypeStruct((SV_DEV, EMB...  21 us
    unnamed x10, local copies, waits for them, and re-layouts  4.89 us

profile of v3, /device:TPU:1, one launch (start us, length us, event | category | flops | bytes accessed | tf_op | source)
XLA Modules:
  0.0 136.6 jit_solution(7526273493544530574)
XLA Ops:
  0.6 0.0 copy-start.3
  0.6 0.9 copy.20.b1
  1.5 0.7 copy.22.b2
  2.3 0.9 copy.23.labels_hbm
  3.2 1.1 copy.18
  4.3 0.3 reshape.13.w1
  4.6 1.3 copy.25
  5.8 0.3 reshape.16.w2
  6.2 0.0 copy-done.3
  6.2 0.0 copy-start.1
  6.2 0.0 copy-start.2
  6.2 1.9 %copy.28 = bf16[48,4,20,256]{3,0,2,1:T(8,128)(2,1)} copy(bf16[48,4,20,256]{3,1,2,0:T(4,128)(2,1)S(1)} %copy-done.3) | data formatting | bytes 3932160 | tf_op args[0]
  8.2 0.0 copy-done.1
  8.2 0.0 copy-done.2
  8.2 104.7 %shard_map.95.got_ref = bf16[128,112,128]{2,1,0:T(8,128)(2,1)} custom-call(bf16[4,20,48,256]{3,2,1,0:T(8,128)(2,1)} %bitcast.9, bf16[144,432]{1,0:T(8,128)(2,1)S(1)} %reshape.13.w1, f32[48,1]{1,0:T(8,128)S(1)} %copy.20.b1, bf16[192,432]{1,0:T(8,128)(2,1)S(1)} %reshape.16.w2, f32[64,1]{1,0:T(8,128)S(1)} %copy.22.b2, s32[256,128]{1,0:T(8,128)S(1)} %bitcast.8, ...), custom_call_target="tpu_custom_call" | custom-call | tf_op jit(solution)/shard_map/pallas_call | solution.py:351
  112.9 0.0 copy-start
  112.9 2.0 %copy-done = bf16[128,112,128]{2,1,0:T(8,128)(2,1)S(1)} copy-done((bf16[128,112,128]{2,1,0:T(8,128)(2,1)S(1)}, bf16[128,112,128]{2,1,0:T(8,128)(2,1)}, u32[]{:S(2)}) %copy-start) | copy-done | bytes 3670040
  114.9 21.0 %shard_map.96 = (f32[128,64]{1,0:T(8,128)S(1)}, f32[128,4096]{1,0:T(8,128)}) custom-call(bf16[128,112,128]{2,1,0:T(8,128)(2,1)S(1)} %copy-done), custom_call_target="tpu_custom_call" | custom-call | tf_op jit(solution)/shard_map/pallas_call | solution.py:607
  135.9 0.7 copy.24
Async XLA Ops:
  0.6 5.6 %copy-start.3 = (bf16[48,4,20,256]{3,1,2,0:T(4,128)(2,1)S(1)}, bf16[48,4,20,256]{3,1,2,0:T(4,128)(2,1)}, u32[]{:S(2)}) copy-start(bf16[48,4,20,256]{3,1,2,0:T(4,128)(2,1)} %param.8) | copy-start | bytes 5898244
  6.2 2.0 %copy-start.1 = (s32[1,1,256,128]{3,2,1,0:T(8,128)S(1)}, s32[1,1,256,128]{3,2,1,0:T(8,128)}, u32[]{:S(2)}) copy-start(s32[1,1,256,128]{3,2,1,0:T(8,128)} %param.14) | copy-start | bytes 393220
  6.2 2.0 %copy-start.2 = (s32[16384]{0:T(1024)S(1)}, s32[16384]{0:T(1024)}, u32[]{:S(2)}) copy-start(s32[16384]{0:T(1024)} %owner_hbm.1) | copy-start | bytes 196612
  112.9 2.0 %copy-start = (bf16[128,112,128]{2,1,0:T(8,128)(2,1)S(1)}, bf16[128,112,128]{2,1,0:T(8,128)(2,1)}, u32[]{:S(2)}) copy-start(bf16[128,112,128]{2,1,0:T(8,128)(2,1)} %shard_map.95.got_ref) | copy-start | bytes 11010052

commit v4 on v3

--- a/solution.py
+++ b/solution.py
@@ -17,6 +17,7 @@
 DEVS = 128
 GROUPS = 160
 AHEAD = 4
+ROUNDS = 7
 MESH = pl.DeviceIdType.MESH
 
 
@@ -76,9 +77,10 @@
 
 
 def main_kernel(
-    own, w1, b1, w2, b2, lists_ref, labels_hbm, owner_hbm, got_ref, wide, hwide, hidden,
+    own, raw1, b1, raw2, b2, lists_ref, labels_hbm, owner_hbm, got_ref, wide, hwide, hidden,
     fz, fy, hz, hy, part1, part2, emb_ref, send_ref, labels_ref, owner_ref, facts, scalars,
     rows_s, rows_v, table_v, table_ref, send_sem, recv_sem, far_send, far_recv, own_sem, here_sem,
+    round_sem, w1, w2,
 ):
     gz, xy = lax.axis_index("gz"), lax.axis_index("xy")
     depth, height = lax.axis_size("gz"), lax.axis_size("xy")
@@ -115,21 +117,36 @@
         ref[e, y, 48:96, :] = value
         ref[e, y, 96:144, :] = right.astype(jnp.bfloat16)
 
-    def greet(k):
+    near = [(a, b) for a in (-1, 0, 1) for b in (-1, 0, 1) if (a, b) != (0, 0)]
+    for a, b in near:
+        there = (gz + a >= 0) & (gz + a < depth) & (xy + b >= 0) & (xy + b < height)
+
+        @pl.when(there)
+        def _():
+            pl.semaphore_signal(
+                barrier, inc=1, device_id=(gz + a, xy + b), device_id_type=MESH
+            )
+
+    def across(r):
+        bit = lax.rem(me // (1 << r), 2)
+        return place(me + (1 - 2 * bit) * (1 << r))
+
+    for r in range(ROUNDS):
+        pl.semaphore_signal(barrier, inc=1, device_id=across(r), device_id_type=MESH)
+
+    def tell(r):
         pl.semaphore_signal(
-            barrier, inc=1, device_id=place(partner(me, k)), device_id_type=MESH
+            round_sem.at[r], inc=1, device_id=across(r), device_id_type=MESH
         )
 
+    def hear(r):
+        pl.semaphore_wait(round_sem.at[r], 1)
+
     def fill(y, carry):
-        for k in range(6):
-            greet(1 + y * 6 + k)
         for z in range(4):
             put(wide, z + 1, y + 1, own[z, y])
         return carry
 
-    lax.fori_loop(0, 20, fill, 0)
-    for k in range(121, DEVS):
-        greet(k)
     count = lists_ref.shape[0]
     lists = lists_ref[...]
     sizes = jnp.sum(jnp.where(lists >= 0, 1, 0), axis=1, keepdims=True)
@@ -137,12 +154,23 @@
     facts[...] = jnp.where(column == 0, lists, sizes).astype(jnp.float32).T[0:8, :].astype(jnp.int32)
     facts_copy = pltpu.make_async_copy(facts, scalars, here_sem.at[2])
     facts_copy.start()
-    pl.semaphore_wait(barrier, DEVS - 1)
+    beside_z = jnp.where(gz > 0, 1, 0) + jnp.where(gz < depth - 1, 1, 0)
+    beside_y = jnp.where(xy > 0, 1, 0) + jnp.where(xy < height - 1, 1, 0)
+    pl.semaphore_wait(barrier, (1 + beside_z) * (1 + beside_y) - 1 + ROUNDS)
 
     first = halo_copies(own, fz, fy, FEATURE_CHUNKS, 0, send_sem, recv_sem)
     then = halo_copies(hidden, hz, hy, HIDDEN_CHUNKS, PER_EXCHANGE, send_sem, recv_sem)
     for entry in first[8:] + first[:8]:
         start(entry)
+    tell(0)
+    for raw, w, channels in ((raw1, w1, 48), (raw2, w2, 64)):
+        for dz in range(3):
+            w[dz * channels : (dz + 1) * channels, :] = jnp.concatenate(
+                [raw[dz * 9 + t] for t in range(9)], axis=1
+            )
+    lax.fori_loop(0, 20, fill, 0)
+    hear(0)
+    tell(1)
 
     def slab(ref, e, y):
         return ref[e, pl.ds(y, 3)].reshape(432, 256)
@@ -167,6 +195,8 @@
 
     for entry in first[8:]:
         arrive(entry)
+    hear(1)
+    tell(2)
 
     def fill_side(e, carry):
         put(wide, e, 0, fy[0, e])
@@ -175,8 +205,13 @@
 
     lax.fori_loop(0, 6, fill_side, 0)
 
-    bias1 = jnp.broadcast_to(b1[...], (48, 256))
-    bias2 = jnp.broadcast_to(b2[...], (64, 256))
+    def bias_of(ref, channels):
+        line = jnp.concatenate([ref[...], jnp.zeros((1, 128 - channels), jnp.float32)], axis=1)
+        tall = jnp.broadcast_to(line, (128, 128)).T[0:channels]
+        return jnp.concatenate([tall, tall], axis=1)
+
+    bias1 = bias_of(b1, 48)
+    bias2 = bias_of(b2, 64)
 
     def keep_hidden(z, y, total):
         value = jnp.maximum(total + bias1, 0.0).astype(jnp.bfloat16)
@@ -251,23 +286,27 @@
         lax.fori_loop(low, low + length, fill_z, 0)
         low, length = HIDDEN_CHUNKS[c]
         lax.fori_loop(low, low + length, first_outer, 0)
-        start(then[2 * c])
-        start(then[2 * c + 1])
         if c == 0:
             for i in (9, 11, 13):
                 start(then[i])
-    for i in (8, 10, 12):
-        start(then[i])
-
-    for entry in then[8:]:
-        arrive(entry)
+        if c == 3:
+            for i in (8, 10, 12):
+                start(then[i])
+        start(then[2 * c])
+        start(then[2 * c + 1])
+        hear(2 + c)
+        tell(3 + c)
+
+    arrive(then[8])
+    arrive(then[9])
+    hear(6)
 
     def hidden_side(e, carry):
         put(hwide, e, 0, hy[0, e])
         put(hwide, e, 21, hy[1, e])
         return carry
 
-    lax.fori_loop(0, 6, hidden_side, 0)
+    lax.fori_loop(1, 5, hidden_side, 0)
 
     def keep(z, y, total):
         value = (total + bias2).astype(jnp.bfloat16)
@@ -295,6 +334,10 @@
         keep(3, y, part2[1, y] + product(w2, hwide, 5, y, 2, 2, 64)[3])
         return carry
 
+    for entry in then[10:]:
+        arrive(entry)
+    hidden_side(0, 0)
+    hidden_side(5, 0)
     for c in range(4):
         arrive(then[2 * c])
         arrive(then[2 * c + 1])
@@ -344,8 +387,8 @@
 
 def main(features, first_weight, first_bias, second_weight, second_bias, labels, blocks, owner_map):
     own = features.transpose(1, 2, 0, 3)
-    w1 = first_weight.transpose(0, 3, 1, 2, 4).reshape(144, 432)
-    w2 = second_weight.transpose(0, 3, 1, 2, 4).reshape(192, 432)
+    w1 = first_weight.reshape(27, 48, 48)
+    w2 = second_weight.reshape(27, 64, 48)
     bf, f32, i32 = jnp.bfloat16, jnp.float32, jnp.int32
     count = blocks.shape[0]
     return pl.pallas_call(
@@ -380,11 +423,14 @@
             pltpu.SemaphoreType.DMA((DEVS,)),
             pltpu.SemaphoreType.DMA,
             pltpu.SemaphoreType.DMA((5,)),
+            pltpu.SemaphoreType.REGULAR((ROUNDS,)),
+            pltpu.VMEM((144, 432), bf),
+            pltpu.VMEM((192, 432), bf),
         ],
         compiler_params=pltpu.CompilerParams(
             collective_id=0, has_side_effects=True, vmem_limit_bytes=52 << 20
         ),
-    )(own, w1, first_bias[:, None], w2, second_bias[:, None], blocks, labels, owner_map)
+    )(own, w1, first_bias[None], w2, second_bias[None], blocks, labels, owner_map)
 
 
 def place(device):
@@ -631,7 +677,7 @@
             pltpu.SemaphoreType.DMA,
             pltpu.SemaphoreType.DMA,
         ],
-        compiler_params=pltpu.CompilerParams(vmem_limit_bytes=48 << 20),
+        compiler_params=pltpu.CompilerParams(vmem_limit_bytes=60 << 20),
     )(got)
 
 

time: 138 us -> 124 us (0.90)
  Pallas kernels: 126 us -> 115 us
  local copies, waits for them, and re-layouts: 10.2 us -> 7.22 us
    pallas_call x1, Pallas kernels: 105 us -> 94.3 us  [main(): pl.pallas_call(main_kernel, out_shape=jax.ShapeDtypeStruct((DEVS, ROWS, 1...]
    reshape x3 -> x0, local copies, waits for them, and re-layouts: 1.83 us -> none  [the longest x2 1.58 us: main(): w2 = second_weight.transpose(0, 3, 1, 2, 4).reshape(192, 432)]
    broadcast_in_dim x2 -> x0, local copies, waits for them, and re-layouts: 1.63 us -> none  [the longest x1 0.88 us: main(): first_bias[:, None]]
    unnamed x10 -> x13, local copies, waits for them, and re-layouts: 4.89 us -> 5.69 us
where the time goes in v4:
time: 124 us; the launch traced here: 123 us
  Pallas kernels  115 us (93%)
  local copies, waits for them, and re-layouts  7.22 us (6%)
    pallas_call x1, Pallas kernels, main(): pl.pallas_call(main_kernel, out_shape=jax.ShapeDtypeStruct((DEVS, ROWS, 1...  94.3 us
    pallas_call x1, Pallas kernels, totals(): pl.pallas_call(total_kernel, out_shape=(jax.ShapeDtypeStruct((SV_DEV, EMB...  20.9 us
    unnamed x13, local copies, waits for them, and re-layouts  5.69 us

profile of v4, /device:TPU:1, one launch (start us, length us, event | category | flops | bytes accessed | tf_op | source)
XLA Modules:
  0.0 123.1 jit_solution(12360806582329215887)
XLA Ops:
  0.6 0.9 copy.12.labels_hbm
  1.5 1.2 copy.11
  2.8 0.0 copy-start
  2.8 0.0 copy-start.1
  2.8 0.0 copy-start.2
  2.8 0.0 copy-start.3
  2.8 0.0 copy-start.4
  2.8 3.5 %copy.15 = bf16[48,4,20,256]{3,0,2,1:T(8,128)(2,1)} copy(bf16[48,4,20,256]{3,1,2,0:T(4,128)(2,1)} %param.8) | data formatting | bytes 3932160 | tf_op args[0]
  6.4 0.0 copy-done
  6.4 0.0 copy-done.1
  6.4 0.0 copy-done.2
  6.4 0.0 copy-done.3
  6.4 0.0 copy-done.4
  6.4 94.3 %shard_map.95.got_ref = bf16[128,112,128]{2,1,0:T(8,128)(2,1)} custom-call(bf16[4,20,48,256]{3,2,1,0:T(8,128)(2,1)} %bitcast.13, bf16[27,48,48]{2,1,0:T(8,128)(2,1)S(1)} %bitcast.9, f32[1,48]{1,0:T(1,128)S(1)} %bitcast.11, bf16[27,64,48]{2,1,0:T(8,128)(2,1)S(1)} %bitcast.8, f32[1,64]{1,0:T(1,128)S(1)} %bitcast.12, s32[256,128]{1,0:T(8,128)S(1)} %bitcast.10, ...), custom_call_target="tpu_custom_call" | custom-call | tf_op jit(solution)/shard_map/pallas_call | solution.py:394
  100.7 20.9 %shard_map.96 = (f32[128,64]{1,0:T(8,128)}, f32[128,4096]{1,0:T(8,128)}) custom-call(bf16[128,112,128]{2,1,0:T(8,128)(2,1)} %shard_map.95.got_ref), custom_call_target="tpu_custom_call" | custom-call | tf_op jit(solution)/shard_map/pallas_call | solution.py:653
  121.6 1.5 %copy.13 = f32[128,64]{0,1:T(8,128)} copy(f32[128,64]{1,0:T(8,128)} %get-tuple-element.2) | data formatting | bytes 65536 | tf_op jit(solution)/shard_map/pallas_call | solution.py:653
Async XLA Ops:
  2.8 3.6 %copy-start = (bf16[3,3,3,48,48]{4,3,2,1,0:T(8,128)(2,1)S(1)}, bf16[3,3,3,48,48]{4,3,2,1,0:T(8,128)(2,1)}, u32[]{:S(2)}) copy-start(bf16[3,3,3,48,48]{4,3,2,1,0:T(8,128)(2,1)} %param.9) | copy-start | bytes 373252
  2.8 3.6 %copy-start.1 = (s32[1,1,256,128]{3,2,1,0:T(8,128)S(1)}, s32[1,1,256,128]{3,2,1,0:T(8,128)}, u32[]{:S(2)}) copy-start(s32[1,1,256,128]{3,2,1,0:T(8,128)} %param.14) | copy-start | bytes 393220
  2.8 3.6 %copy-start.2 = (s32[16384]{0:T(1024)S(1)}, s32[16384]{0:T(1024)}, u32[]{:S(2)}) copy-start(s32[16384]{0:T(1024)} %owner_hbm.1) | copy-start | bytes 196612
  2.8 3.6 %copy-start.3 = (f32[48]{0:T(128)S(1)}, f32[48]{0:T(128)}, u32[]{:S(2)}) copy-start(f32[48]{0:T(128)} %param.10) | copy-start | bytes 580
  2.8 3.6 %copy-start.4 = (f32[64]{0:T(128)S(1)}, f32[64]{0:T(128)}, u32[]{:S(2)}) copy-start(f32[64]{0:T(128)} %param.12) | copy-start | bytes 772

commit v5 on v4

--- a/solution.py
+++ b/solution.py
@@ -218,7 +218,22 @@
         hidden[z, y] = value
         put(hwide, z + 1, y + 1, value)
 
+    labels_copy.wait()
+    owner_copy.wait()
+    facts_copy.wait()
+
+    def look(b):
+        at = scalars[0, b]
+        run = at >> 8
+        z = jnp.clip((run * 3277) >> 16, 0, 3)
+        label = labels_ref[z, jnp.clip(run - z * 20, 0, 19), at & 255]
+        rows_s[0, b] = owner_ref[label & (owner_ref.shape[0] - 1)]
+
+    each = -(-count // 20)
+
     def first_inner(y, carry):
+        for t in range(each):
+            look(jnp.minimum(y * each + t, count - 1))
         total = inner(w1, wide, y, 48)
         part1[0, y] = total[0]
         part1[1, y] = total[3]
@@ -226,21 +241,36 @@
         keep_hidden(2, y, total[2])
         return carry
 
-    lax.fori_loop(0, 20, first_inner, 0, unroll=2)
-
-    labels_copy.wait()
-    owner_copy.wait()
-    facts_copy.wait()
-
-    def look(b, carry):
-        at = scalars[0, b]
-        run = at >> 8
-        z = jnp.clip((run * 3277) >> 16, 0, 3)
-        label = labels_ref[z, jnp.clip(run - z * 20, 0, 19), at & 255]
-        rows_s[0, b] = owner_ref[label & (owner_ref.shape[0] - 1)]
-        return carry
-
-    lax.fori_loop(0, count, look, 0, unroll=8)
+    lax.fori_loop(0, 20, first_inner, 0, unroll=4)
+
+    def fill_z(y, carry):
+        put(wide, 0, y + 1, fz[0, y])
+        put(wide, 5, y + 1, fz[1, y])
+        return carry
+
+    def first_outer(y, carry):
+        keep_hidden(0, y, part1[0, y] + product(w1, wide, 0, y, 0, 0, 48)[0])
+        keep_hidden(3, y, part1[1, y] + product(w1, wide, 5, y, 2, 2, 48)[3])
+        return carry
+
+    for c in range(4):
+        arrive(first[2 * c])
+        arrive(first[2 * c + 1])
+        low, length = FEATURE_CHUNKS[c]
+        lax.fori_loop(low, low + length, fill_z, 0, unroll=length)
+        low, length = HIDDEN_CHUNKS[c]
+        lax.fori_loop(low, low + length, first_outer, 0, unroll=length)
+        if c == 0:
+            for i in (9, 11, 13):
+                start(then[i])
+        if c == 3:
+            for i in (8, 10, 12):
+                start(then[i])
+        start(then[2 * c])
+        start(then[2 * c + 1])
+        hear(2 + c)
+        tell(3 + c)
+
     rows_copy = pltpu.make_async_copy(rows_s, rows_v, here_sem.at[3])
     rows_copy.start()
     rows_copy.wait()
@@ -269,34 +299,6 @@
     table_copy = pltpu.make_async_copy(table_v, table_ref, here_sem.at[4])
     table_copy.start()
 
-    def fill_z(y, carry):
-        put(wide, 0, y + 1, fz[0, y])
-        put(wide, 5, y + 1, fz[1, y])
-        return carry
-
-    def first_outer(y, carry):
-        keep_hidden(0, y, part1[0, y] + product(w1, wide, 0, y, 0, 0, 48)[0])
-        keep_hidden(3, y, part1[1, y] + product(w1, wide, 5, y, 2, 2, 48)[3])
-        return carry
-
-    for c in range(4):
-        arrive(first[2 * c])
-        arrive(first[2 * c + 1])
-        low, length = FEATURE_CHUNKS[c]
-        lax.fori_loop(low, low + length, fill_z, 0)
-        low, length = HIDDEN_CHUNKS[c]
-        lax.fori_loop(low, low + length, first_outer, 0)
-        if c == 0:
-            for i in (9, 11, 13):
-                start(then[i])
-        if c == 3:
-            for i in (8, 10, 12):
-                start(then[i])
-        start(then[2 * c])
-        start(then[2 * c + 1])
-        hear(2 + c)
-        tell(3 + c)
-
     arrive(then[8])
     arrive(then[9])
     hear(6)
@@ -322,7 +324,7 @@
         keep(2, y, total[2])
         return carry
 
-    lax.fori_loop(0, 20, second_inner, 0, unroll=2)
+    lax.fori_loop(0, 20, second_inner, 0, unroll=4)
 
     def hidden_z(y, carry):
         put(hwide, 0, y + 1, hz[0, y])
@@ -342,9 +344,9 @@
         arrive(then[2 * c])
         arrive(then[2 * c + 1])
         low, length = HIDDEN_CHUNKS[c]
-        lax.fori_loop(low, low + length, hidden_z, 0)
+        lax.fori_loop(low, low + length, hidden_z, 0, unroll=length)
         low, length = LAST_CHUNKS[c]
-        lax.fori_loop(low, low + length, second_outer, 0)
+        lax.fori_loop(low, low + length, second_outer, 0, unroll=length)
 
     table_copy.wait()
 
@@ -439,7 +441,7 @@
 
 def partner(me, k):
     core, x, y, z = lax.rem(me, 2), lax.rem(me // 2, 4), lax.rem(me // 8, 4), me // 32
-    kc, kx, ky, kz = lax.rem(k, 2), lax.rem(k // 2, 4), lax.rem(k // 8, 4), k // 32
+    kc, kx, ky, kz = k // 64, lax.rem(k, 4), lax.rem(k // 4, 4), lax.rem(k // 16, 4)
     ky = lax.rem(ky + kx, 4)
     kz = lax.rem(kz + kx + ky, 4)
     there = (lax.rem(z + kz, 4) * 4 + lax.rem(y + ky, 4)) * 4 + lax.rem(x + kx, 4)
@@ -622,7 +624,7 @@
         packed = [
             acc_a[base + t] + pltpu.roll(acc_b[base + t], EMB, 1) for t in range(QUAD)
         ]
-        turned = jnp.concatenate(packed, axis=0).T
+        turned = jnp.concatenate(packed, axis=0).T[0:EMB]
         for t in range(QUAD):
             diag = lines[pl.ds(base + t, 1), :]
             inv = lines[pl.ds(DEVS + base + t, 1), :]
@@ -639,7 +641,7 @@
             full[pl.ds((base + t) * EMB, EMB), :] = both
         return carry
 
-    lax.fori_loop(0, SV_DEV // QUAD, quad, 0)
+    lax.fori_loop(0, SV_DEV // QUAD, quad, 0, unroll=2)
 
     for t in range(EMB // 2):
         even = full[pl.ds(2 * t, SV_DEV, stride=EMB), :]

time: 124 us -> 108 us (0.87)
  Pallas kernels: 115 us -> 99.6 us
    pallas_call x1, Pallas kernels: 94.3 us -> 82.7 us  [main(): pl.pallas_call(main_kernel, out_shape=jax.ShapeDtypeStruct((DEVS, ROWS, 1...]
    pallas_call x1, Pallas kernels: 20.9 us -> 16.9 us  [totals(): pl.pallas_call(total_kernel, out_shape=(jax.ShapeDtypeStruct((SV_DEV, EMB...]
where the time goes in v5:
time: 108 us
  Pallas kernels  99.6 us (92%)
  local copies, waits for them, and re-layouts  7.22 us (7%)
    pallas_call x1, Pallas kernels, main(): pl.pallas_call(main_kernel, out_shape=jax.ShapeDtypeStruct((DEVS, ROWS, 1...  82.7 us
    pallas_call x1, Pallas kernels, totals(): pl.pallas_call(total_kernel, out_shape=(jax.ShapeDtypeStruct((SV_DEV, EMB...  16.9 us
    unnamed x13, local copies, waits for them, and re-layouts  5.69 us

profile of v5, /device:TPU:1, one launch (start us, length us, event | category | flops | bytes accessed | tf_op | source)
XLA Modules:
  0.0 107.5 jit_solution(7868486481280259146)
XLA Ops:
  0.6 0.9 copy.12.labels_hbm
  1.5 1.2 %copy.11 = bf16[3,3,3,64,48]{4,3,2,1,0:T(8,128)(2,1)S(1)} copy(bf16[3,3,3,64,48]{3,4,2,1,0:T(8,128)(2,1)} %param.11) | data formatting | bytes 331776 | tf_op args[3]
  2.8 0.0 copy-start
  2.8 0.0 copy-start.1
  2.8 0.0 copy-start.2
  2.8 0.0 copy-start.3
  2.8 0.0 copy-start.4
  2.8 3.5 %copy.15 = bf16[48,4,20,256]{3,0,2,1:T(8,128)(2,1)} copy(bf16[48,4,20,256]{3,1,2,0:T(4,128)(2,1)} %param.8) | data formatting | bytes 3932160 | tf_op args[0]
  6.4 0.0 copy-done
  6.4 0.0 copy-done.1
  6.4 0.0 copy-done.2
  6.4 0.0 copy-done.3
  6.4 0.0 copy-done.4
  6.4 82.7 %shard_map.95.got_ref = bf16[128,112,128]{2,1,0:T(8,128)(2,1)} custom-call(bf16[4,20,48,256]{3,2,1,0:T(8,128)(2,1)} %bitcast.13, bf16[27,48,48]{2,1,0:T(8,128)(2,1)S(1)} %bitcast.9, f32[1,48]{1,0:T(1,128)S(1)} %bitcast.11, bf16[27,64,48]{2,1,0:T(8,128)(2,1)S(1)} %bitcast.8, f32[1,64]{1,0:T(1,128)S(1)} %bitcast.12, s32[256,128]{1,0:T(8,128)S(1)} %bitcast.10, ...), custom_call_target="tpu_custom_call" | custom-call | tf_op jit(solution)/shard_map/pallas_call | solution.py:396
  89.1 16.9 %shard_map.96 = (f32[128,64]{1,0:T(8,128)}, f32[128,4096]{1,0:T(8,128)}) custom-call(bf16[128,112,128]{2,1,0:T(8,128)(2,1)} %shard_map.95.got_ref), custom_call_target="tpu_custom_call" | custom-call | tf_op jit(solution)/shard_map/pallas_call | solution.py:655
  106.0 1.5 %copy.13 = f32[128,64]{0,1:T(8,128)} copy(f32[128,64]{1,0:T(8,128)} %get-tuple-element.2) | data formatting | bytes 65536 | tf_op jit(solution)/shard_map/pallas_call | solution.py:655
Async XLA Ops:
  2.8 3.6 %copy-start = (bf16[3,3,3,48,48]{4,3,2,1,0:T(8,128)(2,1)S(1)}, bf16[3,3,3,48,48]{4,3,2,1,0:T(8,128)(2,1)}, u32[]{:S(2)}) copy-start(bf16[3,3,3,48,48]{4,3,2,1,0:T(8,128)(2,1)} %param.9) | copy-start | bytes 373252
  2.8 3.6 %copy-start.1 = (s32[1,1,256,128]{3,2,1,0:T(8,128)S(1)}, s32[1,1,256,128]{3,2,1,0:T(8,128)}, u32[]{:S(2)}) copy-start(s32[1,1,256,128]{3,2,1,0:T(8,128)} %param.14) | copy-start | bytes 393220
  2.8 3.6 %copy-start.2 = (s32[16384]{0:T(1024)S(1)}, s32[16384]{0:T(1024)}, u32[]{:S(2)}) copy-start(s32[16384]{0:T(1024)} %owner_hbm.1) | copy-start | bytes 196612
  2.8 3.6 %copy-start.3 = (f32[48]{0:T(128)S(1)}, f32[48]{0:T(128)}, u32[]{:S(2)}) copy-start(f32[48]{0:T(128)} %param.10) | copy-start | bytes 580
  2.8 3.6 %copy-start.4 = (f32[64]{0:T(128)S(1)}, f32[64]{0:T(128)}, u32[]{:S(2)}) copy-start(f32[64]{0:T(128)} %param.12) | copy-start | bytes 772

commit v6 on v5

--- a/solution.py
+++ b/solution.py
@@ -226,7 +226,7 @@
         at = scalars[0, b]
         run = at >> 8
         z = jnp.clip((run * 3277) >> 16, 0, 3)
-        label = labels_ref[z, jnp.clip(run - z * 20, 0, 19), at & 255]
+        label = labels_ref[jnp.clip(run - z * 20, 0, 19), z, at & 255]
         rows_s[0, b] = owner_ref[label & (owner_ref.shape[0] - 1)]
 
     each = -(-count // 20)
@@ -569,7 +569,7 @@
 
     count = jnp.maximum(folded(sums[:, 128:256]), 1.0)
     total_mean = folded(sums[:, 0:128]) / count
-    mean_ref[...] = total_mean[:, 0:EMB]
+    mean_ref[...] = total_mean.T[0:EMB]
     diag_sum = folded(sums[:, 256:384])
     inverse = 1.0 / count
     lines[0:DEVS, :] = diag_sum
@@ -607,7 +607,7 @@
                 acc_b[b] = acc_b[b] + value
             return carry
 
-        lax.fori_loop(c * per, (c + 1) * per, add, 0, unroll=2)
+        lax.fori_loop(c * per, (c + 1) * per, add, 0, unroll=4)
 
     lane32 = lax.broadcasted_iota(jnp.int32, (HALF, 128), 1)
     row32 = lax.broadcasted_iota(jnp.int32, (HALF, 128), 0)
@@ -655,7 +655,7 @@
     return pl.pallas_call(
         total_kernel,
         out_shape=(
-            jax.ShapeDtypeStruct((SV_DEV, EMB), jnp.float32),
+            jax.ShapeDtypeStruct((EMB, SV_DEV), jnp.float32),
             jax.ShapeDtypeStruct((SV_DEV, EMB * EMB), jnp.float32),
         ),
         in_specs=[pl.BlockSpec(memory_space=pl.ANY)],
@@ -692,11 +692,12 @@
         first_bias,
         second_weight,
         second_bias,
-        labels,
+        labels.transpose(1, 0, 2),
         blocks.reshape(blocks.shape[2], blocks.shape[3]),
         owner_map,
     )
-    return totals(got)
+    mean, covariance = totals(got)
+    return mean.T, covariance
 
 
 def solution(mesh):

time: 108 us -> 106 us (0.981)
  local copies, waits for them, and re-layouts: 7.22 us -> 4.79 us
    pallas_call x1 -> x0, local copies, waits for them, and re-layouts: 1.54 us -> none  [totals(): pl.pallas_call(total_kernel, out_shape=(jax.ShapeDtypeStruct((SV_DEV, EMB...]
    unnamed x13 -> x14, local copies, waits for them, and re-layouts: 5.69 us -> 4.79 us
where the time goes in v6:
time: 106 us; the launch traced here: 105 us
  Pallas kernels  99.6 us (94%)
  local copies, waits for them, and re-layouts  4.79 us (5%)
    pallas_call x1, Pallas kernels, main(): pl.pallas_call(main_kernel, out_shape=jax.ShapeDtypeStruct((DEVS, ROWS, 1...  82.7 us
    pallas_call x1, Pallas kernels, totals(): pl.pallas_call(total_kernel, out_shape=(jax.ShapeDtypeStruct((EMB, SV_DEV...  16.9 us
    unnamed x14, local copies, waits for them, and re-layouts  4.79 us

profile of v6, /device:TPU:1, one launch (start us, length us, event | category | flops | bytes accessed | tf_op | source)
XLA Modules:
  0.0 105.3 jit_solution(862183837941996897)
XLA Ops:
  0.6 1.2 %copy.11 = bf16[3,3,3,64,48]{4,3,2,1,0:T(8,128)(2,1)S(1)} copy(bf16[3,3,3,64,48]{3,4,2,1,0:T(8,128)(2,1)} %param.11) | data formatting | bytes 331776 | tf_op args[3]
  1.9 0.0 copy-start
  1.9 0.0 copy-start.1
  1.9 0.0 copy-start.2
  1.9 0.0 copy-start.3
  1.9 0.0 copy-start.4
  1.9 0.0 copy-start.5
  1.9 3.5 %copy.13 = bf16[48,4,20,256]{3,0,2,1:T(8,128)(2,1)} copy(bf16[48,4,20,256]{3,1,2,0:T(4,128)(2,1)} %param.8) | data formatting | bytes 3932160 | tf_op args[0]
  5.5 0.0 copy-done
  5.5 0.0 copy-done.1
  5.5 0.0 copy-done.2
  5.5 0.0 copy-done.3
  5.5 0.0 copy-done.4
  5.5 0.0 copy-done.5
  5.5 82.7 %shard_map.95.got_ref = bf16[128,112,128]{2,1,0:T(8,128)(2,1)} custom-call(bf16[4,20,48,256]{3,2,1,0:T(8,128)(2,1)} %bitcast.16, bf16[27,48,48]{2,1,0:T(8,128)(2,1)S(1)} %bitcast.11, f32[1,48]{1,0:T(1,128)S(1)} %bitcast.14, bf16[27,64,48]{2,1,0:T(8,128)(2,1)S(1)} %bitcast.10, f32[1,64]{1,0:T(1,128)S(1)} %bitcast.15, s32[256,128]{1,0:T(8,128)S(1)} %bitcast.12, ...), custom_call_target="tpu_custom_call" | custom-call | tf_op jit(solution)/shard_map/pallas_call | solution.py:396
  88.2 16.9 %shard_map.96 = (f32[64,128]{1,0:T(8,128)}, f32[128,4096]{1,0:T(8,128)}) custom-call(bf16[128,112,128]{2,1,0:T(8,128)(2,1)} %shard_map.95.got_ref), custom_call_target="tpu_custom_call" | custom-call | tf_op jit(solution)/shard_map/pallas_call | solution.py:655
Async XLA Ops:
  1.9 3.6 %copy-start = (bf16[3,3,3,48,48]{4,3,2,1,0:T(8,128)(2,1)S(1)}, bf16[3,3,3,48,48]{4,3,2,1,0:T(8,128)(2,1)}, u32[]{:S(2)}) copy-start(bf16[3,3,3,48,48]{4,3,2,1,0:T(8,128)(2,1)} %param.9) | copy-start | bytes 373252
  1.9 3.6 %copy-start.1 = (s32[1,1,256,128]{3,2,1,0:T(8,128)S(1)}, s32[1,1,256,128]{3,2,1,0:T(8,128)}, u32[]{:S(2)}) copy-start(s32[1,1,256,128]{3,2,1,0:T(8,128)} %param.14) | copy-start | bytes 393220
  1.9 3.6 %copy-start.2 = (s32[4,20,256]{2,0,1:T(4,128)S(1)}, s32[4,20,256]{2,0,1:T(4,128)}, u32[]{:S(2)}) copy-start(s32[4,20,256]{2,0,1:T(4,128)} %param.13) | copy-start | bytes 245764
  1.9 3.6 %copy-start.3 = (s32[16384]{0:T(1024)S(1)}, s32[16384]{0:T(1024)}, u32[]{:S(2)}) copy-start(s32[16384]{0:T(1024)} %owner_hbm.1) | copy-start | bytes 196612
  1.9 3.6 %copy-start.4 = (f32[48]{0:T(128)S(1)}, f32[48]{0:T(128)}, u32[]{:S(2)}) copy-start(f32[48]{0:T(128)} %param.10) | copy-start | bytes 580
  1.9 3.6 %copy-start.5 = (f32[64]{0:T(128)S(1)}, f32[64]{0:T(128)}, u32[]{:S(2)}) copy-start(f32[64]{0:T(128)} %param.12) | copy-start | bytes 772

commit v7 on v6

--- a/solution.py
+++ b/solution.py
@@ -91,6 +91,46 @@
     labels_copy.start()
     owner_copy.start()
 
+    lane = lax.broadcasted_iota(jnp.int32, (48, 256), 1)
+
+    def put(ref, e, y, value):
+        turned = value.astype(jnp.float32)
+        left = jnp.where(lane == 0, 0.0, pltpu.roll(turned, 1, 1))
+        right = jnp.where(lane == 255, 0.0, pltpu.roll(turned, 255, 1))
+        ref[e, y, 0:48, :] = left.astype(jnp.bfloat16)
+        ref[e, y, 48:96, :] = value
+        ref[e, y, 96:144, :] = right.astype(jnp.bfloat16)
+
+    near = [(a, b) for a in (-1, 0, 1) for b in (-1, 0, 1) if (a, b) != (0, 0)]
+    for a, b in near:
+        there = (gz + a >= 0) & (gz + a < depth) & (xy + b >= 0) & (xy + b < height)
+
+        @pl.when(there)
+        def _():
+            pl.semaphore_signal(
+                barrier, inc=1, device_id=(gz + a, xy + b), device_id_type=MESH
+            )
+
+    def across(r):
+        bit = lax.rem(me // (1 << r), 2)
+        return place(me + (1 - 2 * bit) * (1 << r))
+
+    for r in range(ROUNDS):
+        pl.semaphore_signal(barrier, inc=1, device_id=across(r), device_id_type=MESH)
+
+    def tell(r):
+        pl.semaphore_signal(
+            round_sem.at[r], inc=1, device_id=across(r), device_id_type=MESH
+        )
+
+    def hear(r):
+        pl.semaphore_wait(round_sem.at[r], 1)
+
+    def fill(y, carry):
+        for z in range(4):
+            put(wide, z + 1, y + 1, own[z, y])
+        return carry
+
     for side, has in ((0, gz == 0), (1, gz == depth - 1)):
         @pl.when(has)
         def _():
@@ -107,46 +147,15 @@
             fy[side] = jnp.zeros(fy.shape[1:], fy.dtype)
             hy[side] = jnp.zeros(fy.shape[1:], fy.dtype)
 
-    lane = lax.broadcasted_iota(jnp.int32, (48, 256), 1)
-
-    def put(ref, e, y, value):
-        turned = value.astype(jnp.float32)
-        left = jnp.where(lane == 0, 0.0, pltpu.roll(turned, 1, 1))
-        right = jnp.where(lane == 255, 0.0, pltpu.roll(turned, 255, 1))
-        ref[e, y, 0:48, :] = left.astype(jnp.bfloat16)
-        ref[e, y, 48:96, :] = value
-        ref[e, y, 96:144, :] = right.astype(jnp.bfloat16)
-
-    near = [(a, b) for a in (-1, 0, 1) for b in (-1, 0, 1) if (a, b) != (0, 0)]
-    for a, b in near:
-        there = (gz + a >= 0) & (gz + a < depth) & (xy + b >= 0) & (xy + b < height)
-
-        @pl.when(there)
-        def _():
-            pl.semaphore_signal(
-                barrier, inc=1, device_id=(gz + a, xy + b), device_id_type=MESH
-            )
-
-    def across(r):
-        bit = lax.rem(me // (1 << r), 2)
-        return place(me + (1 - 2 * bit) * (1 << r))
-
-    for r in range(ROUNDS):
-        pl.semaphore_signal(barrier, inc=1, device_id=across(r), device_id_type=MESH)
-
-    def tell(r):
-        pl.semaphore_signal(
-            round_sem.at[r], inc=1, device_id=across(r), device_id_type=MESH
-        )
-
-    def hear(r):
-        pl.semaphore_wait(round_sem.at[r], 1)
-
-    def fill(y, carry):
-        for z in range(4):
-            put(wide, z + 1, y + 1, own[z, y])
-        return carry
-
+    beside_z = jnp.where(gz > 0, 1, 0) + jnp.where(gz < depth - 1, 1, 0)
+    beside_y = jnp.where(xy > 0, 1, 0) + jnp.where(xy < height - 1, 1, 0)
+    pl.semaphore_wait(barrier, (1 + beside_z) * (1 + beside_y) - 1 + ROUNDS)
+
+    first = halo_copies(own, fz, fy, FEATURE_CHUNKS, 0, send_sem, recv_sem)
+    then = halo_copies(hidden, hz, hy, HIDDEN_CHUNKS, PER_EXCHANGE, send_sem, recv_sem)
+    for entry in first[8:] + first[:8]:
+        start(entry)
+    tell(0)
     count = lists_ref.shape[0]
     lists = lists_ref[...]
     sizes = jnp.sum(jnp.where(lists >= 0, 1, 0), axis=1, keepdims=True)
@@ -154,15 +163,6 @@
     facts[...] = jnp.where(column == 0, lists, sizes).astype(jnp.float32).T[0:8, :].astype(jnp.int32)
     facts_copy = pltpu.make_async_copy(facts, scalars, here_sem.at[2])
     facts_copy.start()
-    beside_z = jnp.where(gz > 0, 1, 0) + jnp.where(gz < depth - 1, 1, 0)
-    beside_y = jnp.where(xy > 0, 1, 0) + jnp.where(xy < height - 1, 1, 0)
-    pl.semaphore_wait(barrier, (1 + beside_z) * (1 + beside_y) - 1 + ROUNDS)
-
-    first = halo_copies(own, fz, fy, FEATURE_CHUNKS, 0, send_sem, recv_sem)
-    then = halo_copies(hidden, hz, hy, HIDDEN_CHUNKS, PER_EXCHANGE, send_sem, recv_sem)
-    for entry in first[8:] + first[:8]:
-        start(entry)
-    tell(0)
     for raw, w, channels in ((raw1, w1, 48), (raw2, w2, 64)):
         for dz in range(3):
             w[dz * channels : (dz + 1) * channels, :] = jnp.concatenate(

time: 106 us -> 105 us (level)
  no operation moved by 1% of the time
where the time goes in v7:
time: 105 us
  Pallas kernels  99.5 us (95%)
  local copies, waits for them, and re-layouts  4.79 us (5%)
    pallas_call x1, Pallas kernels, main(): pl.pallas_call(main_kernel, out_shape=jax.ShapeDtypeStruct((DEVS, ROWS, 1...  82.6 us
    pallas_call x1, Pallas kernels, totals(): pl.pallas_call(total_kernel, out_shape=(jax.ShapeDtypeStruct((EMB, SV_DEV...  16.9 us
    unnamed x14, local copies, waits for them, and re-layouts  4.79 us

profile of v7, /device:TPU:1, one launch (start us, length us, event | category | flops | bytes accessed | tf_op | source)
XLA Modules:
  0.0 105.2 jit_solution(3779101908491943313)
XLA Ops:
  0.6 1.2 %copy.11 = bf16[3,3,3,64,48]{4,3,2,1,0:T(8,128)(2,1)S(1)} copy(bf16[3,3,3,64,48]{3,4,2,1,0:T(8,128)(2,1)} %param.11) | data formatting | bytes 331776 | tf_op args[3]
  1.9 0.0 copy-start
  1.9 0.0 copy-start.1
  1.9 0.0 copy-start.2
  1.9 0.0 copy-start.3
  1.9 0.0 copy-start.4
  1.9 0.0 copy-start.5
  1.9 3.5 %copy.13 = bf16[48,4,20,256]{3,0,2,1:T(8,128)(2,1)} copy(bf16[48,4,20,256]{3,1,2,0:T(4,128)(2,1)} %param.8) | data formatting | bytes 3932160 | tf_op args[0]
  5.5 0.0 copy-done
  5.5 0.0 copy-done.1
  5.5 0.0 copy-done.2
  5.5 0.0 copy-done.3
  5.5 0.0 copy-done.4
  5.5 0.0 copy-done.5
  5.5 82.6 %shard_map.95.got_ref = bf16[128,112,128]{2,1,0:T(8,128)(2,1)} custom-call(bf16[4,20,48,256]{3,2,1,0:T(8,128)(2,1)} %bitcast.16, bf16[27,48,48]{2,1,0:T(8,128)(2,1)S(1)} %bitcast.11, f32[1,48]{1,0:T(1,128)S(1)} %bitcast.14, bf16[27,64,48]{2,1,0:T(8,128)(2,1)S(1)} %bitcast.10, f32[1,64]{1,0:T(1,128)S(1)} %bitcast.15, s32[256,128]{1,0:T(8,128)S(1)} %bitcast.12, ...), custom_call_target="tpu_custom_call" | custom-call | tf_op jit(solution)/shard_map/pallas_call | solution.py:396
  88.2 16.9 %shard_map.96 = (f32[64,128]{1,0:T(8,128)}, f32[128,4096]{1,0:T(8,128)}) custom-call(bf16[128,112,128]{2,1,0:T(8,128)(2,1)} %shard_map.95.got_ref), custom_call_target="tpu_custom_call" | custom-call | tf_op jit(solution)/shard_map/pallas_call | solution.py:655
Async XLA Ops:
  1.9 3.6 %copy-start = (bf16[3,3,3,48,48]{4,3,2,1,0:T(8,128)(2,1)S(1)}, bf16[3,3,3,48,48]{4,3,2,1,0:T(8,128)(2,1)}, u32[]{:S(2)}) copy-start(bf16[3,3,3,48,48]{4,3,2,1,0:T(8,128)(2,1)} %param.9) | copy-start | bytes 373252
  1.9 3.6 %copy-start.1 = (s32[1,1,256,128]{3,2,1,0:T(8,128)S(1)}, s32[1,1,256,128]{3,2,1,0:T(8,128)}, u32[]{:S(2)}) copy-start(s32[1,1,256,128]{3,2,1,0:T(8,128)} %param.14) | copy-start | bytes 393220
  1.9 3.6 %copy-start.2 = (s32[4,20,256]{2,0,1:T(4,128)S(1)}, s32[4,20,256]{2,0,1:T(4,128)}, u32[]{:S(2)}) copy-start(s32[4,20,256]{2,0,1:T(4,128)} %param.13) | copy-start | bytes 245764
  1.9 3.6 %copy-start.3 = (s32[16384]{0:T(1024)S(1)}, s32[16384]{0:T(1024)}, u32[]{:S(2)}) copy-start(s32[16384]{0:T(1024)} %owner_hbm.1) | copy-start | bytes 196612
  1.9 3.6 %copy-start.4 = (f32[48]{0:T(128)S(1)}, f32[48]{0:T(128)}, u32[]{:S(2)}) copy-start(f32[48]{0:T(128)} %param.10) | copy-start | bytes 580
  1.9 3.6 %copy-start.5 = (f32[64]{0:T(128)S(1)}, f32[64]{0:T(128)}, u32[]{:S(2)}) copy-start(f32[64]{0:T(128)} %param.12) | copy-start | bytes 772
